TPU v7x, 512 devices: a whole 4x8x8 slice. The times are simulated.
512 devices in a mesh: clip: 8 (over z), guide: 2 (over x_lo), seq: 32 (over y, x_hi, core).
Axes of the slice: x: 4 (x_hi: 2, x_lo: 2; x = x_hi * 2 + x_lo), y: 8, z: 8, core: 2. Of those that a mesh axis runs over, the one named last changes fastest.
Arguments:
- latents: bfloat16 [8, 2, 12288, 1536], P('clip', 'guide', 'seq'), may hold values from -6 to 6
- prompt: bfloat16 [8, 128, 1536], P('clip'), may hold values from -6 to 6
- null_embed: bfloat16 [128, 1536], replicated, may hold values from -6 to 6
- text_lengths: int32 [8], P('clip'), may hold values from 32 to 128, as said below
- timesteps: int32 [8], P('clip'), may hold values from 0 to 49
- head_mod: float32 [50, 2, 1536], replicated, may hold values from -3 to 3
- cross_gain: float32 [1536], replicated, may hold values from 0.1 to 1.9
- cross_bias: float32 [1536], replicated, may hold values from -3 to 3
- q_gain: float32 [1536], replicated, may hold values from 0.1 to 1.9
- k_gain: float32 [1536], replicated, may hold values from 0.1 to 1.9
- w_query: bfloat16 [1536, 1536], P(None, 'seq'), may hold values from -0.15625 to 0.15625
- w_key: bfloat16 [1536, 1536], P(None, 'seq'), may hold values from -0.15625 to 0.15625
- w_value: bfloat16 [1536, 1536], P(None, 'seq'), may hold values from -0.15625 to 0.15625
- w_out: bfloat16 [1536, 1536], P(None, 'seq'), may hold values from -0.15625 to 0.15625
- w_head: bfloat16 [1536, 64], replicated, may hold values from -0.15625 to 0.15625
- head_bias: float32 [64], replicated, may hold values from -3 to 3
- target: bfloat16 [8, 12288, 64], P('clip', 'seq'), may hold values from -6 to 6
Outputs:
- guided: float32 [8, 12288, 64], P('clip', 'seq')
- embed_grad: float32 [8, 2, 128, 1536], P('clip', 'guide', 'seq')
Inputs may be any that keep to these rules, and one draw needn't show every extreme that they name: `text_lengths`: each clip has at least 32 visible prompt tokens; some clip has all 128.
All inputs are finite; a program needn't handle non-finite values.
Results may differ from a plain program's by a relative error of at most 0.0046.
Values may be sent and summed in bfloat16 or wider, within the bound.
A program may use at most 64 MiB of HBM per device.

v0:
```python
import math

import jax
import jax.numpy as jnp
from jax import lax
from jax.sharding import PartitionSpec as P

HEADS = 12


GUIDE_SCALE = 5.0
NORM_EPS = 1e-06


def swapped(block, axis, distance):
    count = lax.axis_size(axis)
    route = []
    for low in range(count):
        high = low | 1 << distance
        if high != low and high < count:
            route += [(low, high), (high, low)]
    return lax.ppermute(block, axis, route)


def layer_norm(values):
    row_mean = jnp.mean(values, axis=-1, keepdims=True)
    centred = values - row_mean
    inverse = lax.rsqrt(jnp.mean(centred * centred, axis=-1, keepdims=True) + NORM_EPS)
    return (centred * inverse, inverse)


def rms_scale(values):
    return lax.rsqrt(jnp.mean(values * values, axis=-1, keepdims=True) + NORM_EPS)


def project(left_rows, block_cols):
    return jnp.dot(left_rows, block_cols, preferred_element_type=jnp.float32)


def on_device(
    latents,
    prompt,
    null_embed,
    text_lengths,
    timesteps,
    head_mod,
    cross_gain,
    cross_bias,
    q_gain,
    k_gain,
    w_query,
    w_key,
    w_value,
    w_out,
    w_head,
    head_bias,
    target,
):
    seq_count = lax.axis_size("seq")
    seq_index = lax.axis_index("seq")
    is_null = lax.axis_index("guide") == 1
    tokens = latents[0, 0]
    row_count = tokens.shape[0]
    model_width = tokens.shape[1]
    text_rows = null_embed.shape[0]
    columns = model_width // seq_count
    head_size = model_width // HEADS
    patch_width = w_head.shape[1]
    context = jnp.where(is_null, null_embed, prompt[0])
    length = jnp.where(is_null, jnp.int32(text_rows), text_lengths[0])
    branch_factor = jnp.where(is_null, 1.0 - GUIDE_SCALE, GUIDE_SCALE)
    key_part = jnp.dot(context, w_key, preferred_element_type=jnp.float32).astype(jnp.bfloat16)
    value_part = jnp.dot(context, w_value, preferred_element_type=jnp.float32).astype(jnp.bfloat16)
    key_raw, value_rows = (
        lax.all_gather(key_part, "seq", axis=1, tiled=True),
        lax.all_gather(value_part, "seq", axis=1, tiled=True),
    )
    key_float = key_raw.astype(jnp.float32)
    key_inverse = rms_scale(key_float)
    key_unit = key_float * key_inverse
    key_normed = (key_unit * k_gain).astype(jnp.bfloat16)
    normed_unit, ignored = layer_norm(tokens.astype(jnp.float32))
    cross_in = (normed_unit * cross_gain + cross_bias).astype(jnp.bfloat16)
    query_raw = project(cross_in, lax.all_gather(w_query, "seq", axis=1, tiled=True))
    out_full = lax.all_gather(w_out, "seq", axis=1, tiled=True)
    query_normed = (query_raw * rms_scale(query_raw) * q_gain).astype(jnp.bfloat16)
    query_heads = query_normed.reshape(row_count, HEADS, head_size)
    key_heads = key_normed.reshape(text_rows, HEADS, head_size)
    value_heads = value_rows.reshape(text_rows, HEADS, head_size)
    scores = jnp.einsum(
        "thd,lhd->htl", query_heads, key_heads, preferred_element_type=jnp.float32
    ) / math.sqrt(head_size)
    visible = jnp.arange(text_rows, dtype=jnp.int32) < length
    masked = jnp.where(visible, scores, -1e30)
    row_max = jnp.max(masked, axis=-1, keepdims=True)
    exp_terms = jnp.where(visible, jnp.exp(masked - row_max), 0.0)
    attn_weights = exp_terms / jnp.sum(exp_terms, axis=-1, keepdims=True)
    weights_half = attn_weights.astype(jnp.bfloat16)
    attended = jnp.einsum(
        "htl,lhd->thd", weights_half, value_heads, preferred_element_type=jnp.float32
    )
    attended = attended.reshape(row_count, model_width).astype(jnp.bfloat16)
    after = tokens.astype(jnp.float32) + jnp.dot(
        attended, out_full, preferred_element_type=jnp.float32
    )
    step_index = timesteps[0]
    step_ids = jnp.arange(head_mod.shape[0], dtype=jnp.int32)
    modulation = jnp.sum(jnp.where(step_ids[:, None, None] == step_index, head_mod, 0.0), axis=0)
    mod_shift = modulation[0]
    mod_scale = modulation[1]
    head_unit, head_inverse = layer_norm(after)
    head_in = (head_unit * (1.0 + mod_scale) + mod_shift).astype(jnp.bfloat16)
    noise_pred = jnp.dot(head_in, w_head, preferred_element_type=jnp.float32) + head_bias
    paired = swapped(noise_pred.reshape(row_count // 2, 2 * patch_width), "guide", 0)
    paired = paired.reshape(row_count, patch_width)
    cond_noise = jnp.where(is_null, paired, noise_pred)
    null_noise = jnp.where(is_null, noise_pred, paired)
    guided = null_noise + GUIDE_SCALE * (cond_noise - null_noise)
    resid = guided - target[0].astype(jnp.float32)
    d_noise = (branch_factor * resid).astype(jnp.bfloat16)
    d_head = jnp.dot(d_noise, w_head.T, preferred_element_type=jnp.float32)
    d_unit = d_head * (1.0 + mod_scale)
    d_after = head_inverse * (
        d_unit
        - jnp.mean(d_unit, axis=-1, keepdims=True)
        - head_unit * jnp.mean(d_unit * head_unit, axis=-1, keepdims=True)
    )
    d_after = d_after.astype(jnp.bfloat16)
    d_attended = jnp.dot(d_after, out_full.T, preferred_element_type=jnp.float32).astype(
        jnp.bfloat16
    )
    d_heads = d_attended.reshape(row_count, HEADS, head_size)
    d_weights = jnp.einsum("thd,lhd->htl", d_heads, value_heads, preferred_element_type=jnp.float32)
    d_scores = attn_weights * (
        d_weights - jnp.sum(d_weights * attn_weights, axis=-1, keepdims=True)
    )
    d_scores = (d_scores / math.sqrt(head_size)).astype(jnp.bfloat16)
    d_keys = jnp.einsum(
        "htl,thd->lhd", d_scores, query_heads, preferred_element_type=jnp.float32
    ).reshape(text_rows, model_width)
    d_values = jnp.einsum(
        "htl,thd->lhd", weights_half, d_heads, preferred_element_type=jnp.float32
    ).reshape(text_rows, model_width)
    first_col = seq_index * columns
    summed_keys, summed_values = lax.psum((d_keys, d_values), "seq")
    gained = summed_keys * k_gain
    statistic = jnp.mean(gained * key_unit, axis=-1, keepdims=True)
    d_key_raw = key_inverse * (gained - key_unit * statistic)
    d_key_cols = lax.dynamic_slice_in_dim(d_key_raw, first_col, columns, 1)
    d_value_cols = lax.dynamic_slice_in_dim(summed_values, first_col, columns, 1)
    key_weight = w_key.astype(jnp.float32).T
    value_weight = w_value.astype(jnp.float32).T
    local_grad = lax.psum_scatter(
        jnp.dot(d_key_cols, key_weight, precision=lax.Precision.HIGHEST)
        + jnp.dot(d_value_cols, value_weight, precision=lax.Precision.HIGHEST),
        "seq",
        scatter_dimension=0,
        tiled=True,
    )
    clip_total = lax.psum(local_grad, "clip")
    embed_rows = jnp.where(is_null, clip_total / lax.axis_size("clip"), local_grad)
    return (guided[None], embed_rows.reshape(1, 1, text_rows // seq_count, model_width))


def solution(mesh):
    return jax.shard_map(
        on_device,
        mesh=mesh,
        in_specs=(
            P("clip", "guide", "seq", None),
            P("clip", None, None),
            P(),
            P("clip"),
            P("clip"),
            P(),
            P(),
            P(),
            P(),
            P(),
            P(None, "seq"),
            P(None, "seq"),
            P(None, "seq"),
            P(None, "seq"),
            P(),
            P(),
            P("clip", "seq", None),
        ),
        out_specs=(P("clip", "seq", None), P("clip", "guide", "seq", None)),
        check_vma=False,
    )
```

profile of v0, /device:TPU:6, one launch (start us, length us, event | category | flops | bytes accessed | tf_op | source)
XLA Modules:
  0.0 830.7 jit_solution(308735671396689557)
XLA Ops:
  7.3 0.7 all-gather.3.cloned.1.call-update
  8.0 0.7 all-gather.5.cloned.1.call-update
  10.1 1.4 select_reduce_fusion
  11.5 1.4 convolution_convert_fusion.2
  12.9 39.7 %all_gather.14 = bf16[128,1536]{0,1:T(8,128)(2,1)S(1)} all-gather(bf16[128,48]{0,1:T(8,128)(2,1)S(1)} %convolution_convert_fusion.2), channel_id=1, replica_groups=mesh['clip'=8,'guide'=2,'seq'=32] {'seq'}, dimensions={1}, use_global_device_ids=true | all-gather | bytes 405504 | tf_op jit(solution)/shard_map/all_gather | solution.py:75
  52.6 0.2 fusion.32
  52.8 0.2 convert_reduce_fusion
  53.1 0.2 convolution_convert_fusion.3
  53.4 42.1 %all_gather.12 = bf16[128,1536]{0,1:T(8,128)(2,1)S(1)} all-gather(bf16[128,48]{0,1:T(8,128)(2,1)S(1)} %convolution_convert_fusion.3), channel_id=1, replica_groups=mesh['clip'=8,'guide'=2,'seq'=32] {'seq'}, dimensions={1}, use_global_device_ids=true | all-gather | bytes 405504 | tf_op jit(solution)/shard_map/all_gather | solution.py:76
  95.5 0.5 fusion.5
  96.0 0.6 copy-done.13
  96.5 1.2 convert_multiply_fusion
  97.7 13.0 %all-gather.3.cloned.1.call-done = bf16[1536,1536]{0,1:T(8,128)(2,1)} async-done(((bf16[1536,48]{0,1:T(8,128)(2,1)}), bf16[1536,1536]{0,1:T(8,128)(2,1)}) %all-gather.3.cloned.1.call-update) | async-done | bytes 4718608 | tf_op jit(solution)/shard_map/all_gather | solution.py:84
  110.8 4.5 multiply_reduce_fusion.3
  115.3 0.3 multiply_convert_fusion.2
  115.5 0.7 copy.40
  116.3 3.9 fusion.59
  120.2 3.3 convolution_convert_fusion.1
  123.4 81.6 %all-gather.5.cloned.1.call-done = bf16[1536,1536]{0,1:T(8,128)(2,1)} async-done(((bf16[1536,48]{0,1:T(8,128)(2,1)}), bf16[1536,1536]{0,1:T(8,128)(2,1)}) %all-gather.5.cloned.1.call-update) | async-done | bytes 4718608 | tf_op jit(solution)/shard_map/all_gather | solution.py:85
  205.1 5.2 fusion.60
  210.2 0.4 multiply_reduce_fusion.2
  210.7 0.2 copy-done.20
  210.9 0.6 fusion.31
  211.6 0.9 copy.44
  212.4 1.0 reshape.104
  213.4 2.1 collective-permute-start
  215.5 4.8 collective-permute-done
  220.4 1.7 reshape.105
  222.1 1.0 copy.45
  223.2 1.8 fusion.58
  225.0 0.6 copy-done.15
  225.5 3.2 convolution_convert_fusion
  228.7 1.7 copy.47
  230.4 1.9 fusion.61
  232.4 0.1 copy-done.21
  232.5 1.6 fusion.33
  234.1 5.6 fusion.14
  239.7 0.0 all-reduce.5.cloned.1.call-start
  239.7 272.3 %all-reduce.7.cloned.1.call-done = (f32[128,1536]{0,1:T(8,128)}, f32[128,1536]{0,1:T(8,128)}) async-done(((f32[128,1536]{0,1:T(8,128)}, f32[128,1536]{0,1:T(8,128)}), (f32[128,1536]{0,1:T(8,128)}, f32[128,1536]{0,1:T(8,128)})) %all-reduce.7.cloned.1.call-update) | async-done | bytes 1572880 | tf_op jit(solution)/shard_map/psum | solution.py:145
  512.1 1.4 multiply_reduce_fusion.4
  513.5 1.3 fusion.44
  514.8 2.2 convolution_add_fusion.1
  517.0 1.3 dynamic-slice
  518.9 0.7 fusion.47
  519.6 271.6 %all-reduce.5.cloned.1.call-done = f32[128,1536]{1,0:T(8,128)} async-done(((f32[128,1536]{1,0:T(8,128)}), f32[128,1536]{1,0:T(8,128)}) %all-reduce.5.cloned.1.call-update) | async-done | bytes 786448
  791.1 0.8 constant_dynamic-slice_fusion
  791.9 30.8 %psum.23 = f32[4,1536]{1,0:T(4,128)S(1)} all-reduce(f32[4,1536]{1,0:T(4,128)S(1)} %constant_dynamic-slice_fusion), channel_id=1, replica_groups=mesh['clip'=8,'guide'=2,'seq'=32] {'clip'}, use_global_device_ids=true, to_apply=%region_16.17 | all-reduce | flops 6144 | bytes 49152 | tf_op jit(solution)/shard_map/psum | solution.py:160
  822.8 1.4 select_bitcast_fusion
  (62 shorter events, 0.4 us)
Async XLA Ops:
  7.2 203.5 %copy-start = (bf16[1536,64]{0,1:T(8,128)(2,1)S(1)}, bf16[1536,64]{0,1:T(8,128)(2,1)}, u32[]{:S(2)}) copy-start(bf16[1536,64]{0,1:T(8,128)(2,1)} %param.31) | copy-start | bytes 589828
  7.2 45.9 %copy-start.16 = (bf16[128,1536]{1,0:T(8,128)(2,1)S(1)}, bf16[128,1536]{1,0:T(8,128)(2,1)}, u32[]{:S(2)}) copy-start(bf16[128,1536]{1,0:T(8,128)(2,1)} %param.19) | copy-start | bytes 1179652
  7.2 45.9 %copy-start.17 = (bf16[1,128,1536]{2,1,0:T(8,128)(2,1)S(1)}, bf16[1,128,1536]{2,1,0:T(8,128)(2,1)}, u32[]{:S(2)}) copy-start(bf16[1,128,1536]{2,1,0:T(8,128)(2,1)} %param.18) | copy-start | bytes 1179652
  7.2 45.6 %copy-start.1 = (bf16[1,1,384,1536]{3,2,1,0:T(8,128)(2,1)S(1)}, bf16[1,1,384,1536]{3,2,1,0:T(8,128)(2,1)}, u32[]{:S(2)}) copy-start(bf16[1,1,384,1536]{3,2,1,0:T(8,128)(2,1)} %param.17) | copy-start | bytes 3538948
  7.2 45.9 %copy-start.4 = (bf16[1536,48]{0,1:T(8,128)(2,1)S(1)}, bf16[1536,48]{0,1:T(8,128)(2,1)}, u32[]{:S(2)}) copy-start(bf16[1536,48]{0,1:T(8,128)(2,1)} %param.29) | copy-start | bytes 442372
  7.2 103.5 %all-gather.3.cloned.1.call-start = ((), (), s32[]{:S(2)}) async-start(), calls=%async_computation | async-start | bytes 4866048 | tf_op jit(solution)/shard_map/all_gather | solution.py:84
  8.0 197.1 %all-gather.5.cloned.1.call-start = ((), (), s32[]{:S(2)}) async-start(), calls=%async_computation.1 | async-start | bytes 4866048 | tf_op jit(solution)/shard_map/all_gather | solution.py:85
  8.7 503.3 %all-reduce.7.cloned.1.call-start = ((), (), s32[]{:S(2)}) async-start(), calls=%async_computation.3 | async-start | bytes 3145728 | tf_op jit(solution)/shard_map/psum | solution.py:145
  12.9 83.6 %copy-start.7 = (f32[1536]{0:T(1024)S(1)}, f32[1536]{0:T(1024)}, u32[]{:S(2)}) copy-start(f32[1536]{0:T(1024)} %param.26) | copy-start | bytes 18436
  53.1 57.7 %copy-start.18 = (f32[1536]{0:T(1024)S(1)}, f32[1536]{0:T(1024)}, u32[]{:S(2)}) copy-start(f32[1536]{0:T(1024)} %param.24) | copy-start | bytes 18436
  53.1 57.6 %copy-start.19 = (f32[1536]{0:T(1024)S(1)}, f32[1536]{0:T(1024)}, u32[]{:S(2)}) copy-start(f32[1536]{0:T(1024)} %param.23) | copy-start | bytes 18436
  95.9 0.6 copy-start.13
  97.7 17.5 %copy-start.10 = (f32[1536]{0:T(1024)S(1)}, f32[1536]{0:T(1024)}, u32[]{:S(2)}) copy-start(f32[1536]{0:T(1024)} %param.25) | copy-start | bytes 18436
  116.3 3.9 copy-start.2
  120.2 3.3 copy-start.22
  210.2 0.7 copy-start.20
  210.2 1.3 copy-start.8
  210.6 0.9 copy-start.11
  213.4 7.0 collective-permute-start
  223.1 1.8 copy-start.9
  223.1 1.8 copy-start.12
  223.2 2.4 copy-start.15
  230.4 2.0 copy-start.21
  230.4 2.0 copy-start.23
  232.5 1.6 copy-start.3
  232.5 1.6 copy-start.24
  234.1 278.0 %copy-start.14 = (f32[128]{0:T(128)S(1)}, f32[128]{0:T(128)}, u32[]{:S(2)}) copy-start(f32[128]{0:T(128)} %copy-done.13) | copy-start | bytes 1540
  239.6 273.8 %copy-start.6 = (bf16[1536,48]{0,1:T(8,128)(2,1)S(1)}, bf16[1536,48]{0,1:T(8,128)(2,1)}, u32[]{:S(2)}) copy-start(bf16[1536,48]{0,1:T(8,128)(2,1)} %param.28) | copy-start | bytes 442372
  239.6 275.1 %copy-start.5 = (bf16[1536,48]{0,1:T(8,128)(2,1)S(1)}, bf16[1536,48]{0,1:T(8,128)(2,1)}, u32[]{:S(2)}) copy-start(bf16[1536,48]{0,1:T(8,128)(2,1)} %param.29) | copy-start | bytes 442372
  239.7 551.5 %all-reduce.5.cloned.1.call-start = ((), (), s32[]{:S(2)}) async-start(), calls=%async_computation.2 | async-start | bytes 1572864
Sparse Core Ops, SparseCore 0:
  11.4 99.2 all-gather.2
  114.1 90.9 all-gather.4
  239.8 272.2 all-reduce.6
  517.1 273.9 all-reduce.4
where the time goes:
time: 835 us; the launch traced here: 831 us
  waiting for transfers between devices  645 us (77%)
  blocking collectives  113 us (14%)
  matrix products  36.5 us (4%)
  between operations  16.1 us (2%)
  local copies, waits for them, and re-layouts  10.7 us (1%)
    unnamed x5, waiting for transfers between devices  273 us
    psum x1, waiting for transfers between devices, on_device(): summed_keys, summed_values = lax.psum((d_keys, d_values), 'seq')  272 us
    all_gather x1, waiting for transfers between devices, on_device(): out_full = lax.all_gather(w_out, 'seq', axis=1, tiled=True)  81.6 us
    all_gather x1, blocking collectives, on_device(): lax.all_gather(value_part, 'seq', axis=1, tiled=True)  42.1 us
    all_gather x1, blocking collectives, on_device(): lax.all_gather(key_part, 'seq', axis=1, tiled=True)  39.7 us
    psum x1, blocking collectives, on_device(): clip_total = lax.psum(local_grad, 'clip')  30.8 us
  transfers between devices with their start and end apart: 5, of which 5 were waited for; matrix products, arithmetic and copies ran while one was open for 2% of the time, Pallas kernels for 0%

commit v1 on v0

v1 whole, which is shorter than its diff:
```python
import functools
import math

import jax
import jax.numpy as jnp
from jax import lax
from jax.experimental import pallas as pl
from jax.experimental.pallas import tpu as pltpu
from jax.sharding import PartitionSpec as P

LANES = 128
GUIDE_SCALE = 5.0
NORM_EPS = 1e-06
GROUP = 4
MESH = pl.DeviceIdType.MESH
F32 = jnp.float32
BF16 = jnp.bfloat16
QUERY, OUT, KEY, VALUE = range(4)


class Place:
    def __init__(self):
        seq = lax.axis_index("seq")
        self.nz = lax.axis_size("clip")
        self.ny = lax.axis_size("seq") // 4
        self.z = lax.axis_index("clip")
        self.xl = lax.axis_index("guide")
        self.y = lax.div(seq, 4)
        self.xh = lax.rem(lax.div(seq, 2), 2)
        self.c = lax.rem(seq, 2)
        self.x = self.xh * 2 + self.xl

    def device(self, z=None, y=None, xh=None, xl=None, c=None):
        z = self.z if z is None else z
        y = self.y if y is None else y
        xh = self.xh if xh is None else xh
        xl = self.xl if xl is None else xl
        c = self.c if c is None else c
        return {"clip": z, "guide": xl, "seq": y * 4 + xh * 2 + c}

    def up_y(self, by):
        return lax.rem(self.y + (by + self.ny), self.ny)

    def up_z(self, by):
        return lax.rem(self.z + (by + self.nz), self.nz)

    def up_x(self, by):
        return lax.rem(self.x + (by + 4), 4)

    def at_y(self, by):
        return self.device(y=self.up_y(by))

    def at_z(self, by):
        return self.device(z=self.up_z(by))

    def at_x(self, by):
        x = self.up_x(by)
        return self.device(xh=lax.div(x, 2), xl=lax.rem(x, 2))

    def sibling(self):
        return self.device(c=1 - self.c)

    def other_columns(self):
        return self.device(xh=1 - self.xh, xl=1 - self.xl)

    def other_tokens(self):
        return self.device(xh=1 - self.xh)

    def other_branch(self):
        return self.device(xl=1 - self.xl)


def remote(src, dst, send_sem, recv_sem, device):
    return pltpu.make_async_remote_copy(
        src_ref=src,
        dst_ref=dst,
        send_sem=send_sem,
        recv_sem=recv_sem,
        device_id=device,
        device_id_type=MESH,
    )


def reach(count):
    return {1: count // 2, -1: count - 1 - count // 2}


class RingY:
    def __init__(self, here, base, partner, recv, send):
        self.here, self.base, self.partner, self.recv, self.send = here, base, partner, recv, send
        hops = reach(here.ny)
        self.hops = {(d, o): hops[d if o == 0 else -d] for d in (1, -1) for o in (0, 1)}
        self.rounds = here.ny // 2

    def chunk(self, y, xh, c):
        return self.base.at[y, xh, c]

    def copy(self, y, xh, c, lane, device):
        ref = self.chunk(y, xh, c)
        return remote(ref, ref, self.send.at[lane], self.recv.at[y * 4 + xh * 2 + c], device)

    def pass_on(self, y, other, step):
        here = self.here
        xh = here.xh if other == 0 else 1 - here.xh
        for d in (1, -1):
            if step == 0 and self.hops[d, other] > 0:
                self.copy(y, xh, here.c, 0, here.at_y(d)).start()
        self.copy(y, xh, here.c, 1, here.sibling()).start()

    def start(self):
        here = self.here
        self.copy(here.y, here.xh, here.c, 2, self.partner).start()
        self.pass_on(here.y, 0, 0)

    def over_x(self):
        here = self.here
        self.copy(here.y, 1 - here.xh, here.c, 2, self.partner).wait_recv()
        self.pass_on(here.y, 1, 0)

    def round(self, k):
        here = self.here
        for other in (0, 1):
            xh = here.xh if other == 0 else 1 - here.xh
            for d in (1, -1):
                if k <= self.hops[d, other]:
                    y = here.up_y(-d * k)
                    self.copy(y, xh, here.c, 0, here.at_y(d)).wait_recv()
                    if k < self.hops[d, other]:
                        self.copy(y, xh, here.c, 0, here.at_y(d)).start()
                    self.copy(y, xh, here.c, 1, here.sibling()).start()

    def from_sibling(self, y):
        here = self.here
        for xh in (0, 1):
            self.copy(y, xh, 1 - here.c, 1, here.sibling()).wait_recv()

    def finish(self):
        here = self.here
        for lane, ref in (
            (0, self.base.at[pl.ds(0, here.ny - 1), :, here.c]),
            (1, self.base.at[:, :, here.c]),
            (2, self.chunk(here.y, here.xh, here.c)),
        ):
            remote(ref, ref, self.send.at[lane], self.recv.at[0], here.sibling()).wait_send()


class RingZ:
    def __init__(self, here, base, first, recv, send):
        self.here, self.base, self.first, self.recv, self.send = here, base, first, recv, send
        self.hops = reach(here.ny)
        hops = reach(here.nz)
        self.z_hops = {(d, h): hops[d if h == 0 else -d] for d in (1, -1) for h in (0, 1)}
        self.rounds = here.ny // 2
        self.z_rounds = here.nz // 2

    def tile(self, z):
        return pl.ds(pl.multiple_of(self.first + z * LANES, LANES), LANES)

    def over(self, xh):
        here = self.here
        ref = self.base.at[here.y, xh, here.c, :, self.tile(here.z)]
        return remote(ref, ref, self.send.at[0], self.recv.at[0], here.other_columns())

    def along(self, y, d):
        here = self.here
        ref = self.base.at[y, :, here.c, :, self.tile(here.z)]
        return remote(ref, ref, self.send.at[1], self.recv.at[1 + y], here.at_y(d))

    def half(self, z, h, c, lane, device):
        size = self.here.ny // 2
        ref = self.base.at[pl.ds(h * size, size), :, c, :, self.tile(z)]
        start = 1 + self.here.ny + (lane - 2) * 2 * self.here.nz
        return remote(ref, ref, self.send.at[lane], self.recv.at[start + z * 2 + h], device)

    def start(self):
        self.over(self.here.xh).start()

    def over_x(self):
        self.over(1 - self.here.xh).wait_recv()
        for d in (1, -1):
            if self.hops[d] > 0:
                self.along(self.here.y, d).start()

    def round(self, k):
        for d in (1, -1):
            if k <= self.hops[d]:
                y = self.here.up_y(-d * k)
                self.along(y, d).wait_recv()
                if k < self.hops[d]:
                    self.along(y, d).start()

    def start_z(self):
        here = self.here
        for h in (0, 1):
            for d in (1, -1):
                if self.z_hops[d, h] > 0:
                    self.half(here.z, h, here.c, 2, here.at_z(d)).start()
        for h in (0, 1):
            self.half(here.z, h, here.c, 3, here.sibling()).start()

    def z_round(self, k):
        here = self.here
        for h in (0, 1):
            for d in (1, -1):
                if k <= self.z_hops[d, h]:
                    z = here.up_z(-d * k)
                    self.half(z, h, here.c, 2, here.at_z(d)).wait_recv()
                    if k < self.z_hops[d, h]:
                        self.half(z, h, here.c, 2, here.at_z(d)).start()
                    self.half(z, h, here.c, 3, here.sibling()).start()

    def from_sibling(self):
        here = self.here
        for z in range(here.nz):
            for h in (0, 1):
                self.half(z, h, 1 - here.c, 3, here.sibling()).wait_recv()

    def finish(self):
        here = self.here
        tiles = here.nz * LANES
        for lane, ref in (
            (0, self.base.at[here.y, here.xh, here.c, :, self.tile(here.z)]),
            (1, self.base.at[pl.ds(0, here.ny - 1), :, here.c, :, self.tile(here.z)]),
            (2, self.base.at[:, :, here.c, :, pl.ds(0, tiles - LANES)]),
            (3, self.base.at[:, :, here.c, :, pl.ds(0, tiles)]),
        ):
            remote(ref, ref, self.send.at[lane], self.recv.at[0], here.sibling()).wait_send()


class RingX:
    def __init__(self, here, base, first, width, recv, send):
        self.here, self.base, self.first, self.width = here, base, first, width
        self.recv, self.send = recv, send
        self.hops = reach(here.ny)
        self.rounds = here.ny // 2

    def part(self, xl):
        return pl.ds(pl.multiple_of(self.first + xl * self.width, LANES), self.width)

    def along(self, y, d):
        here = self.here
        ref = self.base.at[y, here.xh, here.c, :, self.part(here.xl)]
        return remote(ref, ref, self.send.at[0], self.recv.at[y], here.at_y(d))

    def half(self, x, h, c, lane, device):
        size = self.here.ny // 2
        ref = self.base.at[pl.ds(h * size, size), lax.div(x, 2), c, :, self.part(lax.rem(x, 2))]
        start = self.here.ny + (lane - 1) * 8
        return remote(ref, ref, self.send.at[lane], self.recv.at[start + x * 2 + h], device)

    def start(self):
        for d in (1, -1):
            if self.hops[d] > 0:
                self.along(self.here.y, d).start()

    def round(self, k):
        for d in (1, -1):
            if k <= self.hops[d]:
                y = self.here.up_y(-d * k)
                self.along(y, d).wait_recv()
                if k < self.hops[d]:
                    self.along(y, d).start()

    def start_x(self):
        here = self.here
        for h, d in ((0, 1), (1, -1), (1, 1), (0, -1)):
            self.half(here.x, h, here.c, 1, here.at_x(d)).start()
        for h in (0, 1):
            self.half(here.x, h, here.c, 2, here.sibling()).start()

    def x_round(self, k):
        here = self.here
        if k == 1:
            came = ((0, 1, True), (1, -1, True), (1, 1, False), (0, -1, False))
        else:
            came = ((0, 2, False), (1, -2, False))
        for h, d, further in came:
            x = here.up_x(-d)
            toward = here.at_x(1 if d > 0 else -1)
            self.half(x, h, here.c, 1, toward).wait_recv()
            if further:
                self.half(x, h, here.c, 1, toward).start()
            self.half(x, h, here.c, 2, here.sibling()).start()

    def from_sibling(self):
        here = self.here
        for x in range(4):
            for h in (0, 1):
                self.half(jnp.int32(x), h, 1 - here.c, 2, here.sibling()).wait_recv()

    def finish(self):
        here = self.here
        for lane, ref in (
            (0, self.base.at[pl.ds(0, here.ny - 1), 0, here.c, :, pl.ds(0, self.width)]),
            (1, self.base.at[:, 0, here.c, :, pl.ds(0, 3 * self.width)]),
            (2, self.base.at[:, 0, here.c, :, pl.ds(0, 4 * self.width)]),
        ):
            remote(ref, ref, self.send.at[lane], self.recv.at[0], here.sibling()).wait_send()


def down(values):
    return jnp.sum(values, axis=0, keepdims=True)


def dot(left, right):
    return jnp.dot(left, right, preferred_element_type=F32)


def dot_lanes(left, right):
    return lax.dot_general(left, right, (((1,), (1,)), ((), ())), preferred_element_type=F32)


def rows_of(index, size):
    return pl.ds(pl.multiple_of(index * size, size), size)


def kernel(
    length_ref,
    step_ref,
    latents,
    prompt,
    null_embed,
    head_mod,
    cross_gain,
    cross_bias,
    q_gain,
    k_gain,
    w_query,
    w_key,
    w_value,
    w_out,
    w_head,
    head_bias,
    target,
    guided_ref,
    grad_ref,
    weights,
    text,
    context,
    columns,
    w_head_rows,
    tokens,
    cross_in,
    query_raw,
    query,
    key_normed,
    value_rows,
    key_raw,
    attn,
    attended,
    after,
    head_in,
    d_unit,
    d_after,
    d_attended,
    noise,
    d_text,
    d_sibling,
    y_send,
    y_recv,
    x_send,
    x_recv,
    pick,
    core_send,
    core_recv,
    z_send,
    z_recv,
    text_recv,
    text_send,
    query_recv,
    query_send,
    out_z_recv,
    out_z_send,
    out_x_recv,
    out_x_send,
    key_recv,
    key_send,
    value_z_recv,
    value_z_send,
    value_x_recv,
    value_x_send,
    swap_sem,
    sibling_sem,
    y_sem,
    tail_sem,
):
    here = Place()
    ny, nz = here.ny, here.nz
    rows, width = w_query.shape
    token_count = latents.shape[0]
    text_rows = prompt.shape[0]
    heads = width // LANES
    blocks = width // LANES
    token_blocks = token_count // LANES
    band = 4 * rows
    root = 1.0 / math.sqrt(LANES)

    partners = [here.sibling(), here.other_columns(), here.other_tokens(), here.other_branch()]
    partners += [here.at_y(d) for d in range(1, ny)] + [here.at_z(d) for d in range(1, nz)]
    barrier = pltpu.get_barrier_semaphore()
    for device in partners:
        pl.semaphore_signal(barrier, inc=1, device_id=device, device_id_type=MESH)
    z_lanes = nz * LANES
    part = (width - z_lanes) // 2
    for index, own in ((QUERY, w_query), (KEY, w_key)):
        weights[index, here.y, here.xh, here.c] = own[...]
    for index, own in ((OUT, w_out), (VALUE, w_value)):
        for lanes in (
            rows_of(here.z, LANES),
            pl.ds(pl.multiple_of(z_lanes + here.xl * part, LANES), part),
        ):
            weights[index, here.y, here.xh, here.c, :, lanes] = own[:, lanes]
    pl.semaphore_wait(barrier, len(partners))

    text_ring = RingY(here, text, here.other_tokens(), text_recv, text_send)
    query_ring = RingY(here, weights.at[QUERY], here.other_columns(), query_recv, query_send)
    out_z = RingZ(here, weights.at[OUT], 0, out_z_recv, out_z_send)
    out_x = RingX(here, weights.at[OUT], z_lanes, part, out_x_recv, out_x_send)
    key_ring = RingY(here, weights.at[KEY], here.other_columns(), key_recv, key_send)
    value_z = RingZ(here, weights.at[VALUE], 0, value_z_recv, value_z_send)
    value_x = RingX(here, weights.at[VALUE], z_lanes, part, value_x_recv, value_x_send)
    half_y = ny // 2

    out_z.start()
    out_x.start()
    query_ring.start()

    @pl.when(here.xl == 0)
    def _():
        context[...] = prompt[...]

    @pl.when(here.xl == 1)
    def _():
        context[...] = null_embed[...]

    text[here.y, here.xh, here.c, :rows] = dot_lanes(w_key[...], context[...]).astype(BF16)
    text[here.y, here.xh, here.c, rows:] = dot_lanes(w_value[...], context[...]).astype(BF16)
    text_ring.start()
    out_z.over_x()

    modulation = head_mod[step_ref[0]]
    stack = jnp.concatenate(
        [
            cross_gain[...],
            cross_bias[...],
            q_gain[...],
            k_gain[...],
            1.0 + modulation[1:2],
            modulation[0:1],
            jnp.zeros((LANES - 6, width), F32),
        ],
        axis=0,
    )
    for block in range(blocks):
        lanes = slice(block * LANES, (block + 1) * LANES)
        columns[lanes, :] = stack[:, lanes].T
        w_head_rows[lanes, :] = w_head[:, lanes].T

    def turn(block, total):
        at = rows_of(block, LANES)
        for t in range(token_blocks):
            lanes = slice(t * LANES, (t + 1) * LANES)
            tokens[at, lanes] = latents[lanes, at].T
        return total + down(tokens[at, :].astype(F32))

    zero_row = jnp.zeros((1, token_count), F32)
    mean = lax.fori_loop(0, blocks, turn, zero_row) / width

    text_ring.over_x()
    query_ring.over_x()
    out_x.round(1)
    out_z.round(1)

    def spread(block, total):
        centred = tokens[rows_of(block, LANES), :].astype(F32) - mean
        return total + down(centred * centred)

    inverse = lax.rsqrt(lax.fori_loop(0, blocks, spread, zero_row) / width + NORM_EPS)

    def normalise(block, carry):
        at = rows_of(block, LANES)
        unit = (tokens[at, :].astype(F32) - mean) * inverse
        cross_in[at, :] = (unit * columns[at, 0:1] + columns[at, 1:2]).astype(BF16)
        return carry

    lax.fori_loop(0, blocks, normalise, 0)

    def project(y, total):
        raw = dot(weights[QUERY, y].reshape(band, width), cross_in[...])
        query_raw[pl.ds(pl.multiple_of(y * band, 64 if band % 64 == 0 else 16), band), :] = raw
        return total + down(raw * raw)

    def project_round(k, total):
        for d in (1, -1) if 2 * k < ny else (1,):
            query_ring.from_sibling(here.up_y(-d * k))
            total = project(here.up_y(-d * k), total)
        return total

    square = zero_row
    for k in range(1, half_y + 1):
        text_ring.round(k)
        if k > 1:
            out_x.round(k)
            out_z.round(k)
        if k == half_y:
            out_x.start_x()
            out_z.start_z()
        if k == 1:
            query_ring.from_sibling(here.y)
            square = project(here.y, square)
        else:
            square = project_round(k - 1, square)
        query_ring.round(k)
    for y in range(ny):
        text_ring.from_sibling(y)

    def text_block(block):
        per = []
        for start in (0, rows):
            per.append(text[:, :, :, start : start + rows, :].reshape(width, text_rows))
        return per

    keys, values = text_block(0)
    keys = keys.astype(F32)
    key_inverse = lax.rsqrt(down(keys * keys) / width + NORM_EPS)
    for h in range(heads):
        lanes = slice(h * LANES, (h + 1) * LANES)
        one = keys[lanes]
        key_raw[:, lanes] = one.T.astype(BF16)
        key_normed[h] = (one * key_inverse * columns[lanes, 3:4]).T.astype(BF16)
        value_rows[h] = values[lanes].astype(F32).T.astype(BF16)
    value_columns = values

    out_x.x_round(1)
    square = project_round(half_y, square)
    key_ring.start()
    value_z.start()
    value_x.start()
    query_inverse = lax.rsqrt(square / width + NORM_EPS)

    length = here.xl * text_rows + (1 - here.xl) * length_ref[0]
    visible = lax.broadcasted_iota(jnp.int32, (text_rows, token_count), 0) < length

    def attend(h, carry):
        at = rows_of(h, LANES)
        query[at, :] = (query_raw[at, :] * query_inverse * columns[at, 2:3]).astype(BF16)
        scores = dot(key_normed[h], query[at, :]) * root
        masked = jnp.where(visible, scores, -1e30)
        terms = jnp.where(visible, jnp.exp(masked - jnp.max(masked, axis=0, keepdims=True)), 0.0)
        shares = terms / down(terms)
        attn[h] = shares
        attended[at, :] = lax.dot_general(
            value_rows[h],
            shares.astype(BF16),
            (((0,), (0,)), ((), ())),
            preferred_element_type=F32,
        ).astype(BF16)
        return carry

    z_done, x_done = 0, 1
    step = GROUP
    for first in range(0, heads, step):
        lax.fori_loop(first, first + step, attend, 0)
        if z_done < out_z.z_rounds:
            z_done += 1
            out_z.z_round(z_done)
        if x_done < 2:
            x_done += 1
            out_x.x_round(x_done)
        if first == 0:
            key_ring.over_x()
            value_z.over_x()
    while z_done < out_z.z_rounds:
        z_done += 1
        out_z.z_round(z_done)
    value_x.round(1)
    value_z.round(1)
    out_x.from_sibling()
    out_z.from_sibling()

    def project_out(y, total):
        at = pl.ds(pl.multiple_of(y * band, 64 if band % 64 == 0 else 16), band)
        rows_after = dot(weights[OUT, y].reshape(band, width), attended[...]) + tokens[at, :].astype(F32)
        after[at, :] = rows_after
        return total + down(rows_after)

    total = lax.fori_loop(0, half_y, project_out, zero_row)
    key_ring.round(1)
    if half_y > 1:
        value_x.round(2)
        value_z.round(2)
    total = lax.fori_loop(half_y, ny, project_out, total)
    head_mean = total / width

    def head_spread(block, total):
        centred = after[rows_of(block, LANES), :] - head_mean
        return total + down(centred * centred)

    head_inverse = lax.rsqrt(lax.fori_loop(0, blocks, head_spread, zero_row) / width + NORM_EPS)

    def modulate(block, carry):
        at = rows_of(block, LANES)
        unit = (after[at, :] - head_mean) * head_inverse
        head_in[at, :] = (unit * columns[at, 4:5] + columns[at, 5:6]).astype(BF16)
        return carry

    lax.fori_loop(0, blocks, modulate, 0)
    noise[here.xl] = dot(w_head[...], head_in[...]) + head_bias[...]
    swap = remote(
        noise.at[here.xl], noise.at[here.xl], swap_sem.at[0], swap_sem.at[1], here.other_branch()
    )
    swap.start()
    for k in range(3, half_y + 1):
        value_x.round(k)
        value_z.round(k)
    value_x.start_x()
    value_z.start_z()
    if half_y > 1:
        key_ring.round(2)
    swap_back = remote(
        noise.at[1 - here.xl],
        noise.at[1 - here.xl],
        swap_sem.at[0],
        swap_sem.at[1],
        here.other_branch(),
    )
    swap_back.wait_recv()
    swap.wait_send()
    guided = noise[1] + GUIDE_SCALE * (noise[0] - noise[1])
    guided_ref[...] = guided
    factor = GUIDE_SCALE - (2.0 * GUIDE_SCALE - 1.0) * here.xl.astype(F32)
    d_noise = (factor * (guided - target[...].astype(F32))).astype(BF16)

    def head_back(block, sums):
        at = rows_of(block, LANES)
        unit = (after[at, :] - head_mean) * head_inverse
        part_unit = dot(w_head_rows[at, :], d_noise) * columns[at, 4:5]
        d_unit[at, :] = part_unit
        return (sums[0] + down(part_unit), sums[1] + down(part_unit * unit))

    first_sum, second_sum = lax.fori_loop(0, blocks, head_back, (zero_row, zero_row))
    first_mean, second_mean = first_sum / width, second_sum / width

    def norm_back(block, carry):
        at = rows_of(block, LANES)
        unit = (after[at, :] - head_mean) * head_inverse
        grads = (head_inverse * (d_unit[at, :] - first_mean - unit * second_mean)).astype(BF16)
        for t in range(token_blocks):
            lanes = slice(t * LANES, (t + 1) * LANES)
            d_after[lanes, at] = grads[:, lanes].T
        return carry

    lax.fori_loop(0, blocks, norm_back, 0)

    def out_back(block, carry):
        at = rows_of(block, 2 * LANES)
        matrix = weights[OUT, :, :, :, :, at].reshape(width, 2 * LANES)
        d_attended[:, at] = dot(d_after[...], matrix).astype(BF16)
        return carry

    lax.fori_loop(0, blocks // 2, out_back, 0)
    value_x.x_round(1)
    value_z.z_round(1)
    if half_y > 2:
        key_ring.round(3)

    def attend_back(h, carry):
        at = rows_of(h, LANES)
        grads = d_attended[:, at]
        shares = attn[h]
        d_shares = dot_lanes(value_rows[h], grads)
        d_scores = shares * (d_shares - down(d_shares * shares))
        d_text[0, :, at] = dot_lanes((d_scores * root).astype(BF16), query[at, :])
        d_text[1, :, at] = dot(shares.astype(BF16), grads)
        return carry

    groups = heads // GROUP
    wide = GROUP * LANES

    def to_sibling(g):
        lanes = slice(g * wide, (g + 1) * wide)
        return remote(
            d_text.at[1 - here.c, :, lanes],
            d_sibling.at[:, lanes],
            sibling_sem.at[0, g],
            sibling_sem.at[1, g],
            here.sibling(),
        )

    def to_row(g, d):
        lanes = slice(g * wide, (g + 1) * wide)
        return remote(
            y_send.at[here.up_y(d), :, lanes],
            y_recv.at[here.y, :, lanes],
            y_sem.at[0, g],
            y_sem.at[1, g],
            here.at_y(d),
        )

    def sum_cores(g):
        lanes = slice(g * wide, (g + 1) * wide)
        to_sibling(g).wait_recv()
        both = d_text[here.c, :, lanes] + d_sibling[:, lanes]
        d_text[here.c, :, lanes] = both
        y_send[:, :, lanes] = both.astype(BF16).reshape(ny, text_rows // ny, wide)
        for d in range(1, ny):
            to_row(g, d).start()

    for g in range(groups):
        lax.fori_loop(g * GROUP, (g + 1) * GROUP, attend_back, 0)
        to_sibling(g).start()
        if g > 0:
            sum_cores(g - 1)
        if g + 2 <= value_z.z_rounds:
            value_z.z_round(g + 2)
        if g == 0:
            value_x.x_round(2)
    sum_cores(groups - 1)
    for k in range(groups + 2, value_z.z_rounds + 1):
        value_z.z_round(k)
    if half_y > 3:
        key_ring.round(4)

    for g in range(groups):
        lanes = slice(g * wide, (g + 1) * wide)
        ref = y_recv.at[pl.ds(0, ny - 1), :, lanes]
        remote(ref, ref, y_sem.at[0, g], y_sem.at[1, g], here.sibling()).wait_recv()
    share = text_rows // ny
    summed = d_text[here.c, pl.ds(pl.multiple_of(here.y * share, share), share), :]
    for d in range(1, ny):
        summed = summed + y_recv[here.up_y(d)].astype(F32)
    x_send[0] = summed[: share // 2]
    x_send[1] = summed[share // 2 :]
    cross = remote(
        x_send.at[1 - here.xh], x_recv, tail_sem.at[0], tail_sem.at[1], here.other_tokens()
    )
    cross.start()
    for y in range(ny):
        key_ring.from_sibling(y)
    value_x.from_sibling()
    value_z.from_sibling()

    near = key_raw[pl.ds(pl.multiple_of(here.y * share, share), share), :].astype(F32)
    pick[0] = near[: share // 2]
    pick[1] = near[share // 2 :]
    own_keys = pick[here.xh]
    own_inverse = lax.rsqrt(jnp.mean(own_keys * own_keys, axis=-1, keepdims=True) + NORM_EPS)
    own_unit = own_keys * own_inverse
    cross.wait_recv()
    own_sum = x_send[here.xh] + x_recv[...]
    gained = own_sum * k_gain[...]
    statistic = jnp.mean(gained * own_unit, axis=-1, keepdims=True)
    pick[0] = own_inverse * (gained - own_unit * statistic)
    pick[1] = own_sum
    left = pick[here.c]
    high = left.astype(BF16)
    low = (left - high.astype(F32)).astype(BF16)
    both = jnp.concatenate([high, low], axis=0)
    few = share // 2

    def text_back(block, carry):
        at = rows_of(block, 2 * LANES)
        matrix = weights[KEY + here.c, :, :, :, :, at].reshape(width, 2 * LANES)
        product = dot(both, matrix)
        pick[0, :, at] = product[:few] + product[few:]
        return carry

    lax.fori_loop(0, blocks // 2, text_back, 0)
    own_rows = few // 2
    middle = width // 2

    def fold(values):
        return jnp.concatenate([values[:, :middle], values[:, middle:]], axis=0)

    product = pick[0]
    core_send[0] = fold(product[:own_rows])
    core_send[1] = fold(product[own_rows:])
    cores = remote(
        core_send.at[1 - here.c], core_recv, tail_sem.at[2], tail_sem.at[3], here.sibling()
    )
    cores.start()
    cores.wait_recv()
    z_send[...] = core_send[here.c] + core_recv[...]

    def unfold(values):
        grad_ref[:, :middle] = values[:own_rows]
        grad_ref[:, middle:] = values[own_rows:]

    @pl.when(here.xl == 0)
    def _():
        unfold(z_send[...])

    @pl.when(here.xl == 1)
    def _():
        for d in range(1, nz):
            remote(
                z_send, z_recv.at[here.z], tail_sem.at[4], tail_sem.at[5], here.at_z(d)
            ).start()
        ref = z_recv.at[pl.ds(0, nz - 1)]
        gathered = remote(ref, ref, tail_sem.at[4], tail_sem.at[5], here.sibling())
        gathered.wait_recv()
        clips = z_send[...]
        for d in range(1, nz):
            clips = clips + z_recv[here.up_z(d)]
        unfold(clips / nz)
        gathered.wait_send()

    cores.wait_send()
    cross.wait_send()
    for g in range(groups):
        to_sibling(g).wait_send()
        lanes = slice(g * wide, (g + 1) * wide)
        ref = y_send.at[pl.ds(0, ny - 1), :, lanes]
        remote(ref, ref, y_sem.at[0, g], y_sem.at[1, g], here.sibling()).wait_send()
    for ring in (text_ring, query_ring, out_z, out_x, key_ring, value_z, value_x):
        ring.finish()


def on_device(
    latents,
    prompt,
    null_embed,
    text_lengths,
    timesteps,
    head_mod,
    cross_gain,
    cross_bias,
    q_gain,
    k_gain,
    w_query,
    w_key,
    w_value,
    w_out,
    w_head,
    head_bias,
    target,
):
    nz = lax.axis_size("clip")
    ny = lax.axis_size("seq") // 4
    tokens = latents[0, 0]
    count, width = tokens.shape
    text_rows = null_embed.shape[0]
    rows = w_query.shape[1]
    patch = w_head.shape[1]
    heads = width // LANES
    share = text_rows // ny
    own_rows = share // 4
    dma = pltpu.SemaphoreType.DMA
    vmem = pl.BlockSpec(memory_space=pltpu.VMEM)
    smem = pl.BlockSpec(memory_space=pltpu.SMEM)
    z_recvs = 1 + ny + 4 * nz
    x_recvs = ny + 16
    guided, grad = pl.pallas_call(
        kernel,
        out_shape=(
            jax.ShapeDtypeStruct((patch, count), F32),
            jax.ShapeDtypeStruct((own_rows, width), F32),
        ),
        in_specs=[smem, smem] + [vmem] * 15,
        out_specs=(vmem, vmem),
        scratch_shapes=[
            pltpu.VMEM((4, ny, 2, 2, rows, width), BF16),
            pltpu.VMEM((ny, 2, 2, 2 * rows, text_rows), BF16),
            pltpu.VMEM((text_rows, width), BF16),
            pltpu.VMEM((width, LANES), F32),
            pltpu.VMEM((width, patch), BF16),
            pltpu.VMEM((width, count), BF16),
            pltpu.VMEM((width, count), BF16),
            pltpu.VMEM((width, count), F32),
            pltpu.VMEM((width, count), BF16),
            pltpu.VMEM((heads, text_rows, LANES), BF16),
            pltpu.VMEM((heads, text_rows, LANES), BF16),
            pltpu.VMEM((text_rows, width), BF16),
            pltpu.VMEM((heads, text_rows, count), F32),
            pltpu.VMEM((width, count), BF16),
            pltpu.VMEM((width, count), F32),
            pltpu.VMEM((width, count), BF16),
            pltpu.VMEM((width, count), F32),
            pltpu.VMEM((count, width), BF16),
            pltpu.VMEM((count, width), BF16),
            pltpu.VMEM((2, patch, count), F32),
            pltpu.VMEM((2, text_rows, width), F32),
            pltpu.VMEM((text_rows, width), F32),
            pltpu.VMEM((ny, share, width), BF16),
            pltpu.VMEM((ny, share, width), BF16),
            pltpu.VMEM((2, share // 2, width), F32),
            pltpu.VMEM((share // 2, width), F32),
            pltpu.VMEM((2, share // 2, width), F32),
            pltpu.VMEM((2, 2 * own_rows, width // 2), F32),
            pltpu.VMEM((2 * own_rows, width // 2), F32),
            pltpu.VMEM((2 * own_rows, width // 2), F32),
            pltpu.VMEM((nz, 2 * own_rows, width // 2), F32),
            dma((4 * ny,)),
            dma((3,)),
            dma((4 * ny,)),
            dma((3,)),
            dma((z_recvs,)),
            dma((4,)),
            dma((x_recvs,)),
            dma((3,)),
            dma((4 * ny,)),
            dma((3,)),
            dma((z_recvs,)),
            dma((4,)),
            dma((x_recvs,)),
            dma((3,)),
            dma((2,)),
            dma((2, heads // GROUP)),
            dma((2, heads // GROUP)),
            dma((6,)),
        ],
        compiler_params=pltpu.CompilerParams(
            collective_id=0, has_side_effects=True, vmem_limit_bytes=60 * 1024 * 1024
        ),
        cost_estimate=pl.CostEstimate(
            flops=8 * count * width * width, bytes_accessed=8 * count * width, transcendentals=0
        ),
    )(
        text_lengths,
        timesteps,
        tokens,
        prompt[0],
        null_embed,
        head_mod,
        cross_gain.reshape(1, width),
        cross_bias.reshape(1, width),
        q_gain.reshape(1, width),
        k_gain.reshape(1, width),
        w_query.T,
        w_key.T,
        w_value.T,
        w_out.T,
        w_head.T,
        head_bias.reshape(patch, 1),
        target[0].T,
    )
    return (guided.T[None], grad.reshape(1, 1, own_rows, width))


def solution(mesh):
    return jax.shard_map(
        on_device,
        mesh=mesh,
        in_specs=(
            P("clip", "guide", "seq", None),
            P("clip", None, None),
            P(),
            P("clip"),
            P("clip"),
            P(),
            P(),
            P(),
            P(),
            P(),
            P(None, "seq"),
            P(None, "seq"),
            P(None, "seq"),
            P(None, "seq"),
            P(),
            P(),
            P("clip", "seq", None),
        ),
        out_specs=(P("clip", "seq", None), P("clip", "guide", "seq", None)),
        check_vma=False,
    )
```

time: 835 us -> 142 us (0.17)
  waiting for transfers between devices: 645 us -> 0 us
  Pallas kernels: 0 us -> 129 us
  blocking collectives: 113 us -> 0 us
  matrix products: 36.5 us -> 0 us
  between operations: 16.1 us -> 1.93 us
    unnamed x5 -> x0, waiting for transfers between devices: 273 us -> none
    psum x1 -> x0, waiting for transfers between devices: 272 us -> none  [on_device(): summed_keys, summed_values = lax.psum((d_keys, d_values), 'seq')]
    pallas_call x0 -> x1, Pallas kernels: none -> 129 us  [on_device(): pl.pallas_call(kernel, out_shape=(jax.ShapeDtypeStruct((patch, count), F3...]
    all_gather x2 -> x0, waiting for transfers between devices: 94.6 us -> none  [the longest x1 81.6 us: on_device(): out_full = lax.all_gather(w_out, 'seq', axis=1, tiled=True)]
    all_gather x2 -> x0, blocking collectives: 81.8 us -> none  [the longest x1 42.1 us: on_device(): lax.all_gather(value_part, 'seq', axis=1, tiled=True)]
    dot_general x13 -> x0, matrix products: 32.7 us -> none  [the longest x1 5.58 us: on_device(): jnp.einsum('htl,thd->lhd', d_scores, query_heads, preferred_element_type=...]
    psum x1 -> x0, blocking collectives: 30.8 us -> none  [on_device(): clip_total = lax.psum(local_grad, 'clip')]
  transfers between devices with their start and end apart: 5 -> 0, of which waited for: 5 -> 0; matrix products, arithmetic and copies ran while one was open for 2% -> 0% of each run, Pallas kernels for 0% -> 0%
where the time goes in v1:
time: 142 us; the launch traced here: 140 us
  Pallas kernels  129 us (91%)
  local copies, waits for them, and re-layouts  9.41 us (7%)
  between operations  1.93 us (1%)
    pallas_call x1, Pallas kernels, on_device(): pl.pallas_call(kernel, out_shape=(jax.ShapeDtypeStruct((patch, count), F3...  129 us
    unnamed x2, local copies, waits for them, and re-layouts  2.89 us

profile of v1, /device:TPU:6, one launch (start us, length us, event | category | flops | bytes accessed | tf_op | source)
XLA Modules:
  0.0 140.1 jit_solution(7143496733181863313)
XLA Ops:
  1.9 1.3 reshape.22.cross_gain
  3.2 1.3 reshape.23.cross_bias
  4.5 1.3 reshape.24.q_gain
  5.8 1.3 reshape.25.k_gain
  7.1 1.4 copy.19.head_bias
  8.5 128.7 %shard_map.176 = (f32[64,384]{1,0:T(8,128)}, f32[4,1536]{1,0:T(4,128)}) custom-call(s32[1]{0:T(128)S(6)} %copy.22.length_ref, s32[1]{0:T(128)S(6)} %copy.23.step_ref, bf16[384,1536]{1,0:T(8,128)(2,1)} %bitcast.18, bf16[128,1536]{1,0:T(8,128)(2,1)} %bitcast.19, bf16[128,1536]{1,0:T(8,128)(2,1)} %null_embed.1, f32[50,2,1536]{2,1,0:T(2,128)} %head_mod.1, ...), custom_call_target="tpu_custom_call" | custom-call | flops 7247757312 | bytes 4718592 | tf_op jit(solution)/shard_map/pallas_call | solution.py:853
  137.2 1.5 %copy.24 = f32[1,384,64]{1,2,0:T(8,128)} copy(f32[1,384,64]{1,2,0:T(8,128)} %bitcast.15) | data formatting | bytes 196608
  138.7 1.3 copy.25

commit v2 on v1

v2 whole, which is shorter than its diff:
```python
import functools
import math

import jax
import jax.numpy as jnp
from jax import lax
from jax.experimental import pallas as pl
from jax.experimental.pallas import tpu as pltpu
from jax.sharding import PartitionSpec as P

LANES = 128
GUIDE_SCALE = 5.0
NORM_EPS = 1e-06
COLOURS = 4
MESH = pl.DeviceIdType.MESH
F32 = jnp.float32
BF16 = jnp.bfloat16
QUERY, OUT = range(2)


class Place:
    def __init__(self):
        seq = lax.axis_index("seq")
        self.nz = lax.axis_size("clip")
        self.ny = lax.axis_size("seq") // 4
        self.z = lax.axis_index("clip")
        self.xl = lax.axis_index("guide")
        self.y = lax.div(seq, 4)
        self.xh = lax.rem(lax.div(seq, 2), 2)
        self.c = lax.rem(seq, 2)
        self.x = self.xh * 2 + self.xl

    def device(self, z=None, y=None, xh=None, xl=None, c=None):
        z = self.z if z is None else z
        y = self.y if y is None else y
        xh = self.xh if xh is None else xh
        xl = self.xl if xl is None else xl
        c = self.c if c is None else c
        return {"clip": z, "guide": xl, "seq": y * 4 + xh * 2 + c}

    def up_y(self, by):
        return lax.rem(self.y + (by + self.ny), self.ny)

    def up_z(self, by):
        return lax.rem(self.z + (by + self.nz), self.nz)

    def up_x(self, by):
        return lax.rem(self.x + (by + 4), 4)

    def at_y(self, by):
        return self.device(y=self.up_y(by))

    def at_z(self, by):
        return self.device(z=self.up_z(by))

    def at_x(self, by):
        x = self.up_x(by)
        return self.device(xh=lax.div(x, 2), xl=lax.rem(x, 2))

    def sibling(self):
        return self.device(c=1 - self.c)

    def other_columns(self):
        return self.device(xh=1 - self.xh, xl=1 - self.xl)

    def other_tokens(self):
        return self.device(xh=1 - self.xh)

    def other_branch(self):
        return self.device(xl=1 - self.xl)


def remote(src, dst, send_sem, recv_sem, device):
    return pltpu.make_async_remote_copy(
        src_ref=src,
        dst_ref=dst,
        send_sem=send_sem,
        recv_sem=recv_sem,
        device_id=device,
        device_id_type=MESH,
    )


def reach(count):
    return {1: count // 2, -1: count - 1 - count // 2}


class RingY:
    def __init__(self, here, base, lanes, partner, recv, send):
        self.here, self.base, self.lanes, self.partner = here, base, lanes, partner
        self.recv, self.send = recv, send
        hops = reach(here.ny)
        self.hops = {(d, o): hops[d if o == 0 else -d] for d in (1, -1) for o in (0, 1)}
        self.rounds = here.ny // 2

    def chunk(self, y, xh, c):
        return self.base.at[y, xh, c, :, self.lanes]

    def copy(self, y, xh, c, lane, device):
        ref = self.chunk(y, xh, c)
        return remote(ref, ref, self.send.at[lane], self.recv.at[y * 4 + xh * 2 + c], device)

    def pass_on(self, y, other, step):
        here = self.here
        xh = here.xh if other == 0 else 1 - here.xh
        for d in (1, -1):
            if step == 0 and self.hops[d, other] > 0:
                self.copy(y, xh, here.c, 0, here.at_y(d)).start()
        self.copy(y, xh, here.c, 1, here.sibling()).start()

    def start(self):
        here = self.here
        self.copy(here.y, here.xh, here.c, 2, self.partner).start()
        self.pass_on(here.y, 0, 0)

    def over_x(self):
        here = self.here
        self.copy(here.y, 1 - here.xh, here.c, 2, self.partner).wait_recv()
        self.pass_on(here.y, 1, 0)

    def round(self, k):
        here = self.here
        for other in (0, 1):
            xh = here.xh if other == 0 else 1 - here.xh
            for d in (1, -1):
                if k <= self.hops[d, other]:
                    y = here.up_y(-d * k)
                    self.copy(y, xh, here.c, 0, here.at_y(d)).wait_recv()
                    if k < self.hops[d, other]:
                        self.copy(y, xh, here.c, 0, here.at_y(d)).start()
                    self.copy(y, xh, here.c, 1, here.sibling()).start()

    def from_sibling(self, y):
        here = self.here
        for xh in (0, 1):
            self.copy(y, xh, 1 - here.c, 1, here.sibling()).wait_recv()

    def finish(self):
        here = self.here
        for lane, ref in (
            (0, self.base.at[pl.ds(0, here.ny - 1), :, here.c, :, self.lanes]),
            (1, self.base.at[:, :, here.c, :, self.lanes]),
            (2, self.chunk(here.y, here.xh, here.c)),
        ):
            remote(ref, ref, self.send.at[lane], self.recv.at[0], here.sibling()).wait_send()


class RingFour:
    def __init__(self, here, base, first, width, axis, recv, send):
        self.here, self.base, self.first, self.width, self.axis = here, base, first, width, axis
        self.recv, self.send = recv, send
        self.hops = reach(here.ny)
        self.colour = here.x if axis == "x" else lax.rem(here.z, COLOURS)

    def part(self, index):
        return pl.ds(pl.multiple_of(self.first + index * self.width, LANES), self.width)

    def toward(self, d):
        return self.here.at_x(d) if self.axis == "x" else self.here.at_z(d)

    def along(self, y, d):
        here = self.here
        if self.axis == "x":
            ref = self.base.at[y, here.xh, here.c, :, self.part(here.xl)]
        else:
            ref = self.base.at[y, :, here.c, :, self.part(self.colour)]
        return remote(ref, ref, self.send.at[0], self.recv.at[y], here.at_y(d))

    def over(self, xh):
        here = self.here
        ref = self.base.at[here.y, xh, here.c, :, self.part(self.colour)]
        return remote(ref, ref, self.send.at[3], self.recv.at[here.ny + 16], here.other_columns())

    def half(self, colour, h, c, lane, device):
        size = self.here.ny // 2
        span = pl.ds(h * size, size)
        if self.axis == "x":
            ref = self.base.at[span, lax.div(colour, 2), c, :, self.part(lax.rem(colour, 2))]
        else:
            ref = self.base.at[span, :, c, :, self.part(colour)]
        slot = self.here.ny + (lane - 1) * 8 + colour * 2 + h
        return remote(ref, ref, self.send.at[lane], self.recv.at[slot], device)

    def begin_y(self):
        for d in (1, -1):
            if self.hops[d] > 0:
                self.along(self.here.y, d).start()

    def start(self):
        if self.axis == "x":
            self.begin_y()
        else:
            self.over(self.here.xh).start()

    def over_x(self):
        if self.axis == "z":
            self.over(1 - self.here.xh).wait_recv()
            self.begin_y()

    def round(self, k):
        for d in (1, -1):
            if k <= self.hops[d]:
                y = self.here.up_y(-d * k)
                self.along(y, d).wait_recv()
                if k < self.hops[d]:
                    self.along(y, d).start()

    def begin_four(self):
        here = self.here
        for h, d in ((0, 1), (1, -1), (1, 1), (0, -1)):
            self.half(self.colour, h, here.c, 1, self.toward(d)).start()
        for h in (0, 1):
            self.half(self.colour, h, here.c, 2, here.sibling()).start()

    def four(self, k):
        here = self.here
        if k == 1:
            came = ((0, 1, True), (1, -1, True), (1, 1, False), (0, -1, False))
        else:
            came = ((0, 2, False), (1, -2, False))
        for h, d, further in came:
            colour = lax.rem(self.colour + (COLOURS - d), COLOURS)
            toward = self.toward(1 if d > 0 else -1)
            self.half(colour, h, here.c, 1, toward).wait_recv()
            if further:
                self.half(colour, h, here.c, 1, toward).start()
            self.half(colour, h, here.c, 2, here.sibling()).start()

    def from_sibling(self):
        here = self.here
        for colour in range(COLOURS):
            for h in (0, 1):
                self.half(jnp.int32(colour), h, 1 - here.c, 2, here.sibling()).wait_recv()

    def finish(self):
        here = self.here
        xh = 0 if self.axis == "x" else slice(None)
        ends = [
            (0, self.base.at[pl.ds(0, here.ny - 1), xh, here.c, :, pl.ds(0, self.width)]),
            (1, self.base.at[:, xh, here.c, :, pl.ds(0, 3 * self.width)]),
            (2, self.base.at[:, xh, here.c, :, pl.ds(0, 4 * self.width)]),
        ]
        if self.axis == "z":
            ends.append((3, self.base.at[0, 0, here.c, :, pl.ds(0, self.width)]))
        for lane, ref in ends:
            remote(ref, ref, self.send.at[lane], self.recv.at[0], here.sibling()).wait_send()


class Pair:
    def __init__(self, here, base, recv, send):
        self.here, self.base, self.recv, self.send = here, base, recv, send
        self.parity = lax.rem(here.y, 2)
        self.other_y = here.device(y=here.y + 1 - 2 * self.parity)

    def copy(self, parity, xh, c, lane, device):
        ref = self.base.at[:, parity, xh, c]
        slot = parity * 4 + xh * 2 + c
        return remote(ref, ref, self.send.at[lane], self.recv.at[slot], device)

    def start(self):
        here = self.here
        self.copy(self.parity, here.xh, here.c, 2, here.other_columns()).start()
        self.copy(self.parity, here.xh, here.c, 0, self.other_y).start()
        self.copy(self.parity, here.xh, here.c, 1, here.sibling()).start()

    def over_x(self):
        here = self.here
        self.copy(self.parity, 1 - here.xh, here.c, 2, here.other_columns()).wait_recv()
        self.copy(self.parity, 1 - here.xh, here.c, 0, self.other_y).start()
        self.copy(self.parity, 1 - here.xh, here.c, 1, here.sibling()).start()

    def over_y(self):
        here = self.here
        for xh in (here.xh, 1 - here.xh):
            self.copy(1 - self.parity, xh, here.c, 0, self.other_y).wait_recv()
            self.copy(1 - self.parity, xh, here.c, 1, here.sibling()).start()

    def from_sibling(self):
        here = self.here
        for parity in (0, 1):
            for xh in (0, 1):
                self.copy(parity, xh, 1 - here.c, 1, here.sibling()).wait_recv()

    def finish(self):
        here = self.here
        for lane, ref in (
            (0, self.base.at[:, 0, :, here.c]),
            (1, self.base.at[:, :, :, here.c]),
            (2, self.base.at[:, 0, 0, here.c]),
        ):
            remote(ref, ref, self.send.at[lane], self.recv.at[0], here.sibling()).wait_send()


def down(values):
    return jnp.sum(values, axis=0, keepdims=True)


def dot(left, right):
    return jnp.dot(left, right, preferred_element_type=F32)


def dot_lanes(left, right):
    return lax.dot_general(left, right, (((1,), (1,)), ((), ())), preferred_element_type=F32)


def rows_of(index, size):
    return pl.ds(pl.multiple_of(index * size, size), size)


def log2(count):
    return count.bit_length() - 1


def kernel(
    length_ref,
    step_ref,
    latents,
    prompt,
    null_embed,
    head_mod,
    vectors,
    w_query,
    w_key,
    w_value,
    w_out,
    w_head,
    target,
    guided_ref,
    grad_ref,
    weights,
    pair_weights,
    text,
    context,
    columns,
    w_head_rows,
    tokens,
    cross_in,
    query_raw,
    query,
    key_normed,
    value_rows,
    key_raw,
    attn,
    attended,
    after,
    head_in,
    d_unit,
    d_after,
    d_attended,
    noise,
    d_text,
    d_sibling,
    y_send,
    y_recv,
    x_send,
    x_recv,
    product,
    unit_send,
    unit_recv,
    grad_send,
    grad_recv,
    z_send,
    z_recv,
    text_recv,
    text_send,
    recv_y,
    send_y,
    recv_z,
    send_z,
    recv_x,
    send_x,
    pair_recv,
    pair_send,
    swap_sem,
    sibling_sem,
    y_recv_sem,
    y_send_sem,
    tail_sem,
):
    here = Place()
    ny, nz = here.ny, here.nz
    rows, width = w_query.shape
    token_count = latents.shape[0]
    text_rows = prompt.shape[0]
    patch = w_head.shape[0]
    heads = width // LANES
    blocks = width // LANES
    token_blocks = token_count // LANES
    band = 4 * rows
    root = 1.0 / math.sqrt(LANES)
    pairs = ny // 2
    share = text_rows // ny
    own_rows = share // 4
    half, quarter, eighth = text_rows // 2, text_rows // 4, text_rows // 8
    wide = width // pairs
    middle = width // 2
    parity = lax.rem(here.y, 2)
    pair = lax.div(here.y, 2)

    partners = [here.sibling(), here.other_columns(), here.other_tokens(), here.other_branch()]
    partners += [here.at_y(d) for d in range(1, ny)] + [here.at_z(d) for d in range(1, nz)]
    barrier = pltpu.get_barrier_semaphore()
    for device in partners:
        pl.semaphore_signal(barrier, inc=1, device_id=device, device_id_type=MESH)

    x_part = LANES * (2 if blocks >= 12 else 1)
    x_first = width - 2 * x_part
    z_first = x_first - COLOURS * LANES
    y_lanes = pl.ds(0, z_first)
    for index, own in ((QUERY, w_query), (OUT, w_out)):
        for lanes in (
            y_lanes,
            pl.ds(pl.multiple_of(z_first + lax.rem(here.z, COLOURS) * LANES, LANES), LANES),
            pl.ds(pl.multiple_of(x_first + here.xl * x_part, LANES), x_part),
        ):
            weights[index, here.y, here.xh, here.c, :, lanes] = own[:, lanes]
    for index, own in enumerate((w_key, w_value)):
        pair_weights[index, parity, here.xh, here.c] = own[...]
    pl.semaphore_wait(barrier, len(partners))

    text_ring = RingY(here, text, slice(None), here.other_tokens(), text_recv, text_send)
    rings = []
    for index in (QUERY, OUT):
        base = weights.at[index]
        rings.append(
            (
                RingFour(here, base, x_first, x_part, "x", recv_x.at[index], send_x.at[index]),
                RingFour(here, base, z_first, LANES, "z", recv_z.at[index], send_z.at[index]),
                RingY(
                    here, base, y_lanes, here.other_columns(), recv_y.at[index], send_y.at[index]
                ),
            )
        )
    key_value = Pair(here, pair_weights, pair_recv, pair_send)

    def begin(index):
        for ring in rings[index]:
            ring.start()

    def over_x(index):
        for ring in rings[index][1:]:
            ring.over_x()

    def go_round(index, k):
        for ring in rings[index][:2]:
            ring.round(k)
            if k == pairs:
                ring.begin_four()
        rings[index][2].round(k)

    def go_four(index, k):
        for ring in rings[index][:2]:
            ring.four(k)

    def all_here(index):
        for ring in rings[index][:2]:
            ring.from_sibling()
        for y in range(ny):
            rings[index][2].from_sibling(y)

    begin(QUERY)

    def text_row(index):
        place = lax.shift_right_logical(index, log2(own_rows)) & (pairs - 1)
        place = place * 2 + (lax.shift_right_logical(index, log2(quarter)) & 1)
        place = place * 2 + (lax.shift_right_logical(index, log2(eighth)) & 1)
        place = place * 2 + (lax.shift_right_logical(index, log2(half)) & 1)
        return place * own_rows + (index & (own_rows - 1))

    square_iota = functools.partial(lax.broadcasted_iota, jnp.int32, (text_rows, text_rows))
    order = jnp.where(text_row(square_iota(0)) == square_iota(1), 1.0, 0.0).astype(BF16)

    @pl.when(here.xl == 0)
    def _():
        context[...] = dot(order, prompt[...]).astype(BF16)

    @pl.when(here.xl == 1)
    def _():
        context[...] = dot(order, null_embed[...]).astype(BF16)

    text[here.y, here.xh, here.c, :rows] = dot_lanes(w_key[...], context[...]).astype(BF16)
    text[here.y, here.xh, here.c, rows:] = dot_lanes(w_value[...], context[...]).astype(BF16)
    text_ring.start()
    over_x(QUERY)

    modulation = head_mod[step_ref[0]]
    stack = jnp.concatenate(
        [
            vectors[...],
            1.0 + modulation[1:2],
            modulation[0:1],
            jnp.zeros((LANES - 10, width), F32),
        ],
        axis=0,
    )
    for block in range(blocks):
        lanes = slice(block * LANES, (block + 1) * LANES)
        columns[lanes, :] = stack[:, lanes].T
        w_head_rows[lanes, :] = w_head[:, lanes].T

    def turn(block, total):
        at = rows_of(block, LANES)
        for t in range(token_blocks):
            lanes = slice(t * LANES, (t + 1) * LANES)
            tokens[at, lanes] = latents[lanes, at].T
        return total + down(tokens[at, :].astype(F32))

    zero_row = jnp.zeros((1, token_count), F32)
    mean = lax.fori_loop(0, blocks, turn, zero_row) / width

    go_round(QUERY, 1)
    text_ring.over_x()
    begin(OUT)

    def spread(block, total):
        centred = tokens[rows_of(block, LANES), :].astype(F32) - mean
        return total + down(centred * centred)

    inverse = lax.rsqrt(lax.fori_loop(0, blocks, spread, zero_row) / width + NORM_EPS)

    def normalise(block, carry):
        at = rows_of(block, LANES)
        unit = (tokens[at, :].astype(F32) - mean) * inverse
        cross_in[at, :] = (unit * columns[at, 0:1] + columns[at, 1:2]).astype(BF16)
        return carry

    lax.fori_loop(0, blocks, normalise, 0)

    if pairs > 1:
        go_round(QUERY, 2)
    text_ring.round(1)
    over_x(OUT)
    for k in range(3, pairs + 1):
        go_round(QUERY, k)
        text_ring.round(k - 1)
        go_round(OUT, k - 2)
    go_four(QUERY, 1)
    if pairs > 1:
        text_ring.round(pairs)
    for k in range(max(1, pairs - 1), pairs):
        go_round(OUT, k)
    go_four(QUERY, 2)
    go_round(OUT, pairs)
    for y in range(ny):
        text_ring.from_sibling(y)

    keys = text[:, :, :, :rows, :].reshape(width, text_rows).astype(F32)
    values = text[:, :, :, rows:, :].reshape(width, text_rows).astype(F32)
    key_inverse = lax.rsqrt(down(keys * keys) / width + NORM_EPS)
    for h in range(heads):
        lanes = slice(h * LANES, (h + 1) * LANES)
        one = keys[lanes]
        key_raw[:, lanes] = one.T.astype(BF16)
        key_normed[h] = (one * key_inverse * columns[lanes, 3:4]).T.astype(BF16)
        value_rows[h] = values[lanes].T.astype(BF16)

    all_here(QUERY)

    def project(y, total):
        raw = dot(weights[QUERY, y].reshape(band, width), cross_in[...])
        query_raw[rows_of(y, band), :] = raw
        return total + down(raw * raw)

    square = lax.fori_loop(0, ny, project, zero_row)
    go_four(OUT, 1)
    query_inverse = lax.rsqrt(square / width + NORM_EPS)

    length = here.xl * text_rows + (1 - here.xl) * length_ref[0]
    visible = text_row(lax.broadcasted_iota(jnp.int32, (text_rows, token_count), 0)) < length

    def attend(h, carry):
        at = rows_of(h, LANES)
        query[at, :] = (query_raw[at, :] * query_inverse * columns[at, 2:3]).astype(BF16)
        scores = dot(key_normed[h], query[at, :]) * root
        masked = jnp.where(visible, scores, -1e30)
        terms = jnp.where(visible, jnp.exp(masked - jnp.max(masked, axis=0, keepdims=True)), 0.0)
        shares = terms / down(terms)
        attn[h] = shares
        attended[at, :] = lax.dot_general(
            value_rows[h],
            shares.astype(BF16),
            (((0,), (0,)), ((), ())),
            preferred_element_type=F32,
        ).astype(BF16)
        return carry

    lax.fori_loop(0, heads // 2, attend, 0)
    go_four(OUT, 2)
    key_value.start()
    lax.fori_loop(heads // 2, heads, attend, 0)
    all_here(OUT)

    def project_out(y, total):
        at = rows_of(y, band)
        rows_after = dot(weights[OUT, y].reshape(band, width), attended[...]) + tokens[at, :].astype(F32)
        after[at, :] = rows_after
        return total + down(rows_after)

    head_mean = lax.fori_loop(0, ny, project_out, zero_row) / width

    def head_spread(block, total):
        centred = after[rows_of(block, LANES), :] - head_mean
        return total + down(centred * centred)

    head_inverse = lax.rsqrt(lax.fori_loop(0, blocks, head_spread, zero_row) / width + NORM_EPS)

    def modulate(block, carry):
        at = rows_of(block, LANES)
        unit = (after[at, :] - head_mean) * head_inverse
        head_in[at, :] = (unit * columns[at, 8:9] + columns[at, 9:10]).astype(BF16)
        return carry

    lax.fori_loop(0, blocks, modulate, 0)
    noise[here.xl] = dot(w_head[...], head_in[...]) + columns[:patch, 4:5]

    def swap(branch):
        ref = noise.at[branch]
        return remote(ref, ref, swap_sem.at[0], swap_sem.at[1], here.other_branch())

    swap(here.xl).start()
    key_value.over_x()

    def fold(values):
        return jnp.concatenate([values[:, :middle], values[:, middle:]], axis=0)

    def split(values):
        high = values.astype(BF16)
        low = (values - high.astype(F32)).astype(BF16)
        return jnp.concatenate([high, low], axis=0)

    first_row = here.c * half + parity * quarter + here.xh * eighth
    own_span = pl.ds(pl.multiple_of(first_row, eighth), eighth)
    own_lanes = rows_of(pair, wide)
    near = key_raw[own_span, :].astype(F32)
    near_inverse = lax.rsqrt(jnp.mean(near * near, axis=-1, keepdims=True) + NORM_EPS)
    near_unit = key_raw[own_span, own_lanes].astype(F32) * near_inverse

    def multiply(left, lead):
        both = split(left)

        def columns_of(block, carry):
            at = rows_of(block, 2 * LANES)
            if lead:
                matrix = pair_weights[:, :, :, :, :, at].reshape(2 * wide, 2 * LANES)
            else:
                matrix = pair_weights[0, :, :, :, :, at].reshape(wide, 2 * LANES)
            result = dot(both, matrix)
            product[:, at] = result[:eighth] + result[eighth:]
            return carry

        lax.fori_loop(0, blocks // 2, columns_of, 0)

    def exchange(send, recv, lane):
        for d in range(1, pairs):
            q = lax.rem(pair + d, pairs)
            remote(
                send.at[q],
                recv.at[pair],
                tail_sem.at[lane],
                tail_sem.at[lane + 1],
                here.device(y=q * 2 + parity),
            ).start()
        ref = recv.at[pl.ds(0, max(1, pairs - 1))]
        return remote(ref, ref, tail_sem.at[lane], tail_sem.at[lane + 1], here.sibling())

    def collect(send, recv):
        total = send[pair]
        for d in range(1, pairs):
            total = total + recv[lax.rem(pair + d, pairs)]
        return total

    swap(1 - here.xl).wait_recv()
    swap(here.xl).wait_send()
    guided = noise[1] + GUIDE_SCALE * (noise[0] - noise[1])
    guided_ref[...] = guided
    factor = GUIDE_SCALE - (2.0 * GUIDE_SCALE - 1.0) * here.xl.astype(F32)
    d_noise = (factor * (guided - target[...].astype(F32))).astype(BF16)

    def head_back(block, sums):
        at = rows_of(block, LANES)
        unit = (after[at, :] - head_mean) * head_inverse
        part_unit = dot(w_head_rows[at, :], d_noise) * columns[at, 8:9]
        d_unit[at, :] = part_unit
        return (sums[0] + down(part_unit), sums[1] + down(part_unit * unit))

    first_sum, second_sum = lax.fori_loop(0, blocks, head_back, (zero_row, zero_row))
    first_mean, second_mean = first_sum / width, second_sum / width

    def norm_back(block, carry):
        at = rows_of(block, LANES)
        unit = (after[at, :] - head_mean) * head_inverse
        grads = (head_inverse * (d_unit[at, :] - first_mean - unit * second_mean)).astype(BF16)
        for t in range(token_blocks):
            lanes = slice(t * LANES, (t + 1) * LANES)
            d_after[lanes, at] = grads[:, lanes].T
        return carry

    lax.fori_loop(0, blocks, norm_back, 0)

    def out_back(block, carry):
        at = rows_of(block, 2 * LANES)
        matrix = weights[OUT, :, :, :, :, at].reshape(width, 2 * LANES)
        d_attended[:, at] = dot(d_after[...], matrix).astype(BF16)
        return carry

    lax.fori_loop(0, blocks // 2, out_back, 0)
    key_value.over_y()

    def attend_back(h, carry):
        at = rows_of(h, LANES)
        grads = d_attended[:, at]
        shares = attn[h]
        d_shares = dot_lanes(value_rows[h], grads)
        d_scores = shares * (d_shares - down(d_shares * shares))
        d_text[0, :, at] = dot_lanes((d_scores * root).astype(BF16), query[at, :])
        d_text[1, :, at] = dot(shares.astype(BF16), grads)
        return carry

    def group(i):
        return lax.rem(pair + (i + 1), pairs)

    def core_span(c):
        return pl.ds(pl.multiple_of(c * half, half), half)

    def to_sibling(i):
        lanes = rows_of(group(i), wide)
        return remote(
            d_text.at[:, core_span(1 - here.c), lanes],
            d_sibling.at[:, :, lanes],
            sibling_sem.at[0, i],
            sibling_sem.at[1, i],
            here.sibling(),
        )

    def to_row(i, odd):
        lanes = rows_of(group(i), wide)
        span = pl.ds(pl.multiple_of(odd * quarter, quarter), quarter)
        return remote(
            y_send.at[:, span, lanes],
            y_recv.at[here.y],
            y_send_sem.at[i],
            y_recv_sem.at[here.y],
            here.device(y=group(i) * 2 + odd),
        )

    def sum_cores(i):
        lanes = rows_of(group(i), wide)
        to_sibling(i).wait_recv()
        both = d_text[:, core_span(here.c), lanes] + d_sibling[:, :, lanes]
        y_send[:, :, lanes] = both.astype(BF16)
        if i < pairs - 1:
            for odd in (0, 1):
                to_row(i, jnp.int32(odd)).start()
        else:
            to_row(i, 1 - parity).start()
            d_sibling[:, :, lanes] = both

    for i in range(pairs):
        first = group(i) * (heads // pairs)
        lax.fori_loop(first, first + heads // pairs, attend_back, 0)
        to_sibling(i).start()
        if i > 0:
            sum_cores(i - 1)
        if i == pairs - 2 or pairs == 1:
            key_value.from_sibling()
            multiply(near_unit * near_inverse, False)
            for q in range(pairs):
                unit_send[q] = fold(product[q * own_rows : (q + 1) * own_rows, :])
            units = exchange(unit_send, unit_recv, 2)
    sum_cores(pairs - 1)

    quarter_span = pl.ds(pl.multiple_of(parity * quarter, quarter), quarter)
    summed = d_sibling[:, quarter_span, own_lanes]
    for d in list(range(2, ny)) + [0]:
        y = lax.rem(pair * 2 + d, ny) if d else here.y + 1 - 2 * parity
        ref = y_recv.at[y]
        remote(ref, ref, y_send_sem.at[0], y_recv_sem.at[y], here.sibling()).wait_recv()
        summed = summed + y_recv[y].astype(F32)
    x_send[0] = summed[:, :eighth]
    x_send[1] = summed[:, eighth:]
    cross = remote(
        x_send.at[1 - here.xh], x_recv, tail_sem.at[0], tail_sem.at[1], here.other_tokens()
    )
    cross.start()
    if pairs > 1:
        units.wait_recv()
    unit_total = collect(unit_send, unit_recv)
    own_gain = vectors[3:4, own_lanes]
    cross.wait_recv()
    own_sum = x_send[here.xh] + x_recv[...]
    gained = own_sum[0] * own_gain
    statistic = jnp.sum(gained * near_unit, axis=-1, keepdims=True) / width
    multiply(jnp.concatenate([near_inverse * gained, own_sum[1]], axis=1), True)
    for q in range(pairs):
        span = slice(q * own_rows, (q + 1) * own_rows)
        grad_send[q, :, :middle] = fold(product[span, :])
        both = jnp.broadcast_to(statistic[span], (own_rows, LANES))
        grad_send[q, :, middle:] = jnp.concatenate([both, both], axis=0)
    grads = exchange(grad_send, grad_recv, 4)
    if pairs > 1:
        grads.wait_recv()
    total = collect(grad_send, grad_recv)
    z_send[...] = total[:, :middle] - total[:, middle : middle + 1] * unit_total

    def unfold(values):
        grad_ref[:, :middle] = values[:own_rows]
        grad_ref[:, middle:] = values[own_rows:]

    @pl.when(here.xl == 0)
    def _():
        unfold(z_send[...])

    @pl.when(here.xl == 1)
    def _():
        for d in range(1, nz):
            remote(
                z_send, z_recv.at[here.z], tail_sem.at[6], tail_sem.at[7], here.at_z(d)
            ).start()
        ref = z_recv.at[pl.ds(0, nz - 1)]
        gathered = remote(ref, ref, tail_sem.at[6], tail_sem.at[7], here.sibling())
        gathered.wait_recv()
        clips = z_send[...]
        for d in range(1, nz):
            clips = clips + z_recv[here.up_z(d)]
        unfold(clips / nz)
        gathered.wait_send()

    cross.wait_send()
    if pairs > 1:
        units.wait_send()
        grads.wait_send()
    for i in range(pairs):
        to_sibling(i).wait_send()
        ref = y_send.at[:, :, rows_of(group(i), wide)]
        if i == pairs - 1:
            ref = y_send.at[:, pl.ds(0, quarter), rows_of(group(i), wide)]
        remote(ref, ref, y_send_sem.at[i], y_recv_sem.at[0], here.sibling()).wait_send()
    text_ring.finish()
    key_value.finish()
    for three in rings:
        for ring in three:
            ring.finish()


def on_device(
    latents,
    prompt,
    null_embed,
    text_lengths,
    timesteps,
    head_mod,
    cross_gain,
    cross_bias,
    q_gain,
    k_gain,
    w_query,
    w_key,
    w_value,
    w_out,
    w_head,
    head_bias,
    target,
):
    nz = lax.axis_size("clip")
    ny = lax.axis_size("seq") // 4
    tokens = latents[0, 0]
    count, width = tokens.shape
    text_rows = null_embed.shape[0]
    rows = w_query.shape[1]
    patch = w_head.shape[1]
    heads = width // LANES
    pairs = ny // 2
    wide = width // pairs
    middle = width // 2
    half, quarter, eighth = text_rows // 2, text_rows // 4, text_rows // 8
    own_rows = text_rows // ny // 4
    dma = pltpu.SemaphoreType.DMA
    vmem = pl.BlockSpec(memory_space=pltpu.VMEM)
    smem = pl.BlockSpec(memory_space=pltpu.SMEM)
    vectors = jnp.stack(
        [cross_gain, cross_bias, q_gain, k_gain, jnp.pad(head_bias, (0, width - patch))]
        + [jnp.zeros_like(k_gain)] * 3
    )
    guided, grad = pl.pallas_call(
        kernel,
        out_shape=(
            jax.ShapeDtypeStruct((patch, count), F32),
            jax.ShapeDtypeStruct((own_rows, width), F32),
        ),
        in_specs=[smem, smem] + [vmem] * 11,
        out_specs=(vmem, vmem),
        scratch_shapes=[
            pltpu.VMEM((2, ny, 2, 2, rows, width), BF16),
            pltpu.VMEM((2, 2, 2, 2, rows, width), BF16),
            pltpu.VMEM((ny, 2, 2, 2 * rows, text_rows), BF16),
            pltpu.VMEM((text_rows, width), BF16),
            pltpu.VMEM((width, LANES), F32),
            pltpu.VMEM((width, patch), BF16),
            pltpu.VMEM((width, count), BF16),
            pltpu.VMEM((width, count), BF16),
            pltpu.VMEM((width, count), F32),
            pltpu.VMEM((width, count), BF16),
            pltpu.VMEM((heads, text_rows, LANES), BF16),
            pltpu.VMEM((heads, text_rows, LANES), BF16),
            pltpu.VMEM((text_rows, width), BF16),
            pltpu.VMEM((heads, text_rows, count), F32),
            pltpu.VMEM((width, count), BF16),
            pltpu.VMEM((width, count), F32),
            pltpu.VMEM((width, count), BF16),
            pltpu.VMEM((width, count), F32),
            pltpu.VMEM((count, width), BF16),
            pltpu.VMEM((count, width), BF16),
            pltpu.VMEM((2, patch, count), F32),
            pltpu.VMEM((2, text_rows, width), F32),
            pltpu.VMEM((2, half, width), F32),
            pltpu.VMEM((2, half, width), BF16),
            pltpu.VMEM((ny, 2, quarter, wide), BF16),
            pltpu.VMEM((2, 2, eighth, wide), F32),
            pltpu.VMEM((2, eighth, wide), F32),
            pltpu.VMEM((eighth, width), F32),
            pltpu.VMEM((pairs, 2 * own_rows, middle), F32),
            pltpu.VMEM((pairs, 2 * own_rows, middle), F32),
            pltpu.VMEM((pairs, 2 * own_rows, middle + LANES), F32),
            pltpu.VMEM((pairs, 2 * own_rows, middle + LANES), F32),
            pltpu.VMEM((2 * own_rows, middle), F32),
            pltpu.VMEM((nz, 2 * own_rows, middle), F32),
            dma((4 * ny,)),
            dma((3,)),
            dma((2, 4 * ny)),
            dma((2, 3)),
            dma((2, ny + 17)),
            dma((2, 4)),
            dma((2, ny + 16)),
            dma((2, 3)),
            dma((8,)),
            dma((3,)),
            dma((2,)),
            dma((2, pairs)),
            dma((ny,)),
            dma((pairs,)),
            dma((8,)),
        ],
        compiler_params=pltpu.CompilerParams(
            collective_id=0, has_side_effects=True, vmem_limit_bytes=60 * 1024 * 1024
        ),
        cost_estimate=pl.CostEstimate(
            flops=8 * count * width * width, bytes_accessed=8 * count * width, transcendentals=0
        ),
    )(
        text_lengths,
        timesteps,
        tokens,
        prompt[0],
        null_embed,
        head_mod,
        vectors,
        w_query.T,
        w_key.T,
        w_value.T,
        w_out.T,
        w_head.T,
        target[0].T,
    )
    return (guided.T[None], grad.reshape(1, 1, own_rows, width))


def solution(mesh):
    return jax.shard_map(
        on_device,
        mesh=mesh,
        in_specs=(
            P("clip", "guide", "seq", None),
            P("clip", None, None),
            P(),
            P("clip"),
            P("clip"),
            P(),
            P(),
            P(),
            P(),
            P(),
            P(None, "seq"),
            P(None, "seq"),
            P(None, "seq"),
            P(None, "seq"),
            P(),
            P(),
            P("clip", "seq", None),
        ),
        out_specs=(P("clip", "seq", None), P("clip", "guide", "seq", None)),
        check_vma=False,
    )
```

time: 142 us -> 121 us (0.85); the launches traced: 140 us -> 121 us
  Pallas kernels: 129 us -> 112 us
  local copies, waits for them, and re-layouts: 9.41 us -> 7.06 us
    pallas_call x1, Pallas kernels: 129 us -> 112 us  [on_device(): pl.pallas_call(kernel, out_shape=(jax.ShapeDtypeStruct((patch, count), F3...]
    reshape x5 -> x0, local copies, waits for them, and re-layouts: 6.53 us -> none  [the longest x1 1.36 us: on_device(): head_bias.reshape(patch, 1)]
    another operation x0 -> x8, local copies, waits for them, and re-layouts: none -> 3.51 us  [on_device(): jnp.stack([cross_gain, cross_bias, q_gain, k_gain, jnp.pad(head_bias, (0,...]
where the time goes in v2:
time: 121 us
  Pallas kernels  112 us (93%)
  local copies, waits for them, and re-layouts  7.06 us (6%)
  between operations  1.95 us (2%)
    pallas_call x1, Pallas kernels, on_device(): pl.pallas_call(kernel, out_shape=(jax.ShapeDtypeStruct((patch, count), F3...  112 us
    another operation x8, local copies, waits for them, and re-layouts, on_device(): jnp.stack([cross_gain, cross_bias, q_gain, k_gain, jnp.pad(head_bias, (0,...  3.51 us
    unnamed x2, local copies, waits for them, and re-layouts  2.89 us

profile of v2, /device:TPU:6, one launch (start us, length us, event | category | flops | bytes accessed | tf_op | source)
XLA Modules:
  0.0 121.0 jit_solution(4117183871961115034)
XLA Ops:
  1.9 0.7 stack.21
  2.6 0.7 stack.22
  3.3 0.7 stack.23
  4.0 0.7 stack.24
  4.7 0.7 pad.4
  5.4 0.7 stack.27.vectors
  6.1 112.0 %shard_map.176 = (f32[64,384]{1,0:T(8,128)}, f32[4,1536]{1,0:T(4,128)}) custom-call(s32[1]{0:T(128)S(6)} %copy.21.length_ref, s32[1]{0:T(128)S(6)} %copy.22.step_ref, bf16[384,1536]{1,0:T(8,128)(2,1)} %bitcast.16, bf16[128,1536]{1,0:T(8,128)(2,1)} %bitcast.17, bf16[128,1536]{1,0:T(8,128)(2,1)} %null_embed.1, f32[50,2,1536]{2,1,0:T(2,128)} %head_mod.1, ...), custom_call_target="tpu_custom_call" | custom-call | flops 7247757312 | bytes 4718592 | tf_op jit(solution)/shard_map/pallas_call | solution.py:884
  118.2 1.5 %copy.23 = f32[1,384,64]{1,2,0:T(8,128)} copy(f32[1,384,64]{1,2,0:T(8,128)} %bitcast.14) | data formatting | bytes 196608
  119.7 1.3 %copy.24 = f32[1,1,4,1536]{3,2,1,0:T(4,128)} copy(f32[1,1,4,1536]{3,2,1,0:T(4,128)} %bitcast.15) | data formatting | bytes 49152
  (3 shorter events, 0.0 us)

commit v3 on v2

--- a/solution.py
+++ b/solution.py
@@ -303,6 +303,10 @@
     return lax.dot_general(left, right, (((1,), (1,)), ((), ())), preferred_element_type=F32)
 
 
+def row(ref):
+    return ref[...].reshape(1, ref.shape[0])
+
+
 def rows_of(index, size):
     return pl.ds(pl.multiple_of(index * size, size), size)
 
@@ -314,19 +318,28 @@
 def kernel(
     length_ref,
     step_ref,
-    latents,
-    prompt,
-    null_embed,
-    head_mod,
-    vectors,
+    latents_in,
+    prompt_in,
+    null_in,
+    head_mod_in,
+    cross_gain,
+    cross_bias,
+    q_gain,
+    k_gain,
     w_query,
     w_key,
     w_value,
     w_out,
+    w_head_in,
+    head_bias,
+    target_in,
+    guided_ref,
+    grad_ref,
+    latents,
+    either,
+    head_mod,
     w_head,
     target,
-    guided_ref,
-    grad_ref,
     weights,
     pair_weights,
     text,
@@ -355,6 +368,7 @@
     x_send,
     x_recv,
     product,
+    lane_gain,
     unit_send,
     unit_recv,
     grad_send,
@@ -376,13 +390,14 @@
     y_recv_sem,
     y_send_sem,
     tail_sem,
+    load_sem,
 ):
     here = Place()
     ny, nz = here.ny, here.nz
     rows, width = w_query.shape
-    token_count = latents.shape[0]
-    text_rows = prompt.shape[0]
-    patch = w_head.shape[0]
+    token_count = latents_in.shape[0]
+    text_rows = prompt_in.shape[0]
+    patch = w_head_in.shape[0]
     heads = width // LANES
     blocks = width // LANES
     token_blocks = token_count // LANES
@@ -407,15 +422,40 @@
     x_first = width - 2 * x_part
     z_first = x_first - COLOURS * LANES
     y_lanes = pl.ds(0, z_first)
+    loads = []
+
+    def load(src, dst):
+        loads.append(pltpu.make_async_copy(src, dst, load_sem.at[len(loads)]))
+        loads[-1].start()
+
     for index, own in ((QUERY, w_query), (OUT, w_out)):
         for lanes in (
             y_lanes,
             pl.ds(pl.multiple_of(z_first + lax.rem(here.z, COLOURS) * LANES, LANES), LANES),
             pl.ds(pl.multiple_of(x_first + here.xl * x_part, LANES), x_part),
         ):
-            weights[index, here.y, here.xh, here.c, :, lanes] = own[:, lanes]
+            load(own.at[:, lanes], weights.at[index, here.y, here.xh, here.c, :, lanes])
     for index, own in enumerate((w_key, w_value)):
-        pair_weights[index, parity, here.xh, here.c] = own[...]
+        load(own, pair_weights.at[index, parity, here.xh, here.c])
+    for src, dst in (
+        (head_mod_in, head_mod),
+        (w_head_in, w_head),
+        (latents_in, latents),
+        (target_in, target),
+    ):
+        load(src, dst)
+    text_load = load_sem.at[len(loads)]
+
+    @pl.when(here.xl == 0)
+    def _():
+        pltpu.make_async_copy(prompt_in, either, text_load).start()
+
+    @pl.when(here.xl == 1)
+    def _():
+        pltpu.make_async_copy(null_in, either, text_load).start()
+
+    for copy in loads[:6]:
+        copy.wait()
     pl.semaphore_wait(barrier, len(partners))
 
     text_ring = RingY(here, text, slice(None), here.other_tokens(), text_recv, text_send)
@@ -433,20 +473,14 @@
         )
     key_value = Pair(here, pair_weights, pair_recv, pair_send)
 
-    def begin(index):
-        for ring in rings[index]:
-            ring.start()
-
-    def over_x(index):
-        for ring in rings[index][1:]:
-            ring.over_x()
-
-    def go_round(index, k):
+    x_query, z_query, y_query = rings[QUERY]
+    x_out, z_out, y_out = rings[OUT]
+
+    def small_round(index, k):
         for ring in rings[index][:2]:
             ring.round(k)
             if k == pairs:
                 ring.begin_four()
-        rings[index][2].round(k)
 
     def go_four(index, k):
         for ring in rings[index][:2]:
@@ -458,7 +492,8 @@
         for y in range(ny):
             rings[index][2].from_sibling(y)
 
-    begin(QUERY)
+    for ring in rings[QUERY]:
+        ring.start()
 
     def text_row(index):
         place = lax.shift_right_logical(index, log2(own_rows)) & (pairs - 1)
@@ -470,26 +505,31 @@
     square_iota = functools.partial(lax.broadcasted_iota, jnp.int32, (text_rows, text_rows))
     order = jnp.where(text_row(square_iota(0)) == square_iota(1), 1.0, 0.0).astype(BF16)
 
-    @pl.when(here.xl == 0)
-    def _():
-        context[...] = dot(order, prompt[...]).astype(BF16)
-
-    @pl.when(here.xl == 1)
-    def _():
-        context[...] = dot(order, null_embed[...]).astype(BF16)
-
-    text[here.y, here.xh, here.c, :rows] = dot_lanes(w_key[...], context[...]).astype(BF16)
-    text[here.y, here.xh, here.c, rows:] = dot_lanes(w_value[...], context[...]).astype(BF16)
+    pltpu.make_async_copy(prompt_in, either, text_load).wait()
+    context[...] = dot(order, either[...]).astype(BF16)
+    for copy in loads[6:8]:
+        copy.wait()
+    own_key = pair_weights[0, parity, here.xh, here.c]
+    own_value = pair_weights[1, parity, here.xh, here.c]
+    text[here.y, here.xh, here.c, :rows] = dot_lanes(own_key, context[...]).astype(BF16)
+    text[here.y, here.xh, here.c, rows:] = dot_lanes(own_value, context[...]).astype(BF16)
     text_ring.start()
-    over_x(QUERY)
-
+    z_query.over_x()
+    y_query.over_x()
+
+    for copy in loads[8:]:
+        copy.wait()
     modulation = head_mod[step_ref[0]]
     stack = jnp.concatenate(
         [
-            vectors[...],
+            row(cross_gain),
+            row(cross_bias),
+            row(q_gain),
+            row(k_gain),
             1.0 + modulation[1:2],
             modulation[0:1],
-            jnp.zeros((LANES - 10, width), F32),
+            jnp.concatenate([row(head_bias), jnp.zeros((1, width - patch), F32)], axis=1),
+            jnp.zeros((LANES - 7, width), F32),
         ],
         axis=0,
     )
@@ -508,9 +548,10 @@
     zero_row = jnp.zeros((1, token_count), F32)
     mean = lax.fori_loop(0, blocks, turn, zero_row) / width
 
-    go_round(QUERY, 1)
+    small_round(QUERY, 1)
     text_ring.over_x()
-    begin(OUT)
+    x_out.start()
+    z_out.start()
 
     def spread(block, total):
         centred = tokens[rows_of(block, LANES), :].astype(F32) - mean
@@ -524,23 +565,42 @@
         cross_in[at, :] = (unit * columns[at, 0:1] + columns[at, 1:2]).astype(BF16)
         return carry
 
+    y_query.round(1)
+    z_out.over_x()
+    if pairs > 1:
+        small_round(QUERY, 2)
+    text_ring.round(1)
     lax.fori_loop(0, blocks, normalise, 0)
 
+    y_out.start()
+    for k in range(3, pairs + 1):
+        small_round(QUERY, k)
+        small_round(OUT, k - 2)
+        if k == 3:
+            y_out.over_x()
+            y_query.round(2)
+            text_ring.round(2)
+    if pairs < 3:
+        y_out.over_x()
+        if pairs > 1:
+            y_query.round(2)
+            text_ring.round(2)
+    if pairs > 2:
+        y_query.round(3)
+        text_ring.round(3)
     if pairs > 1:
-        go_round(QUERY, 2)
-    text_ring.round(1)
-    over_x(OUT)
-    for k in range(3, pairs + 1):
-        go_round(QUERY, k)
-        text_ring.round(k - 1)
-        go_round(OUT, k - 2)
+        small_round(OUT, pairs - 1)
+        y_out.round(1)
     go_four(QUERY, 1)
+    small_round(OUT, pairs)
+    if pairs > 3:
+        text_ring.round(4)
+        y_query.round(4)
     if pairs > 1:
-        text_ring.round(pairs)
-    for k in range(max(1, pairs - 1), pairs):
-        go_round(OUT, k)
+        y_out.round(2)
+    else:
+        y_out.round(1)
     go_four(QUERY, 2)
-    go_round(OUT, pairs)
     for y in range(ny):
         text_ring.from_sibling(y)
 
@@ -561,8 +621,11 @@
         query_raw[rows_of(y, band), :] = raw
         return total + down(raw * raw)
 
-    square = lax.fori_loop(0, ny, project, zero_row)
+    square = lax.fori_loop(0, ny // 2, project, zero_row)
     go_four(OUT, 1)
+    if pairs > 2:
+        y_out.round(3)
+    square = lax.fori_loop(ny // 2, ny, project, square)
     query_inverse = lax.rsqrt(square / width + NORM_EPS)
 
     length = here.xl * text_rows + (1 - here.xl) * length_ref[0]
@@ -584,10 +647,13 @@
         ).astype(BF16)
         return carry
 
-    lax.fori_loop(0, heads // 2, attend, 0)
+    lax.fori_loop(0, heads // 4, attend, 0, unroll=True)
     go_four(OUT, 2)
+    lax.fori_loop(heads // 4, heads // 2, attend, 0, unroll=True)
+    if pairs > 3:
+        y_out.round(4)
     key_value.start()
-    lax.fori_loop(heads // 2, heads, attend, 0)
+    lax.fori_loop(heads // 2, heads, attend, 0, unroll=True)
     all_here(OUT)
 
     def project_out(y, total):
@@ -607,11 +673,11 @@
     def modulate(block, carry):
         at = rows_of(block, LANES)
         unit = (after[at, :] - head_mean) * head_inverse
-        head_in[at, :] = (unit * columns[at, 8:9] + columns[at, 9:10]).astype(BF16)
+        head_in[at, :] = (unit * columns[at, 4:5] + columns[at, 5:6]).astype(BF16)
         return carry
 
     lax.fori_loop(0, blocks, modulate, 0)
-    noise[here.xl] = dot(w_head[...], head_in[...]) + columns[:patch, 4:5]
+    noise[here.xl] = dot(w_head[...], head_in[...]) + columns[:patch, 6:7]
 
     def swap(branch):
         ref = noise.at[branch]
@@ -679,7 +745,7 @@
     def head_back(block, sums):
         at = rows_of(block, LANES)
         unit = (after[at, :] - head_mean) * head_inverse
-        part_unit = dot(w_head_rows[at, :], d_noise) * columns[at, 8:9]
+        part_unit = dot(w_head_rows[at, :], d_noise) * columns[at, 4:5]
         d_unit[at, :] = part_unit
         return (sums[0] + down(part_unit), sums[1] + down(part_unit * unit))
 
@@ -756,8 +822,8 @@
             d_sibling[:, :, lanes] = both
 
     for i in range(pairs):
-        first = group(i) * (heads // pairs)
-        lax.fori_loop(first, first + heads // pairs, attend_back, 0)
+        for j in range(heads // pairs):
+            attend_back(group(i) * (heads // pairs) + j, 0)
         to_sibling(i).start()
         if i > 0:
             sum_cores(i - 1)
@@ -785,7 +851,8 @@
     if pairs > 1:
         units.wait_recv()
     unit_total = collect(unit_send, unit_recv)
-    own_gain = vectors[3:4, own_lanes]
+    lane_gain[...] = row(k_gain)
+    own_gain = lane_gain[:, own_lanes]
     cross.wait_recv()
     own_sum = x_send[here.xh] + x_recv[...]
     gained = own_sum[0] * own_gain
@@ -800,7 +867,7 @@
     if pairs > 1:
         grads.wait_recv()
     total = collect(grad_send, grad_recv)
-    z_send[...] = total[:, :middle] - total[:, middle : middle + 1] * unit_total
+    own_grad = total[:, :middle] - total[:, middle : middle + 1] * unit_total
 
     def unfold(values):
         grad_ref[:, :middle] = values[:own_rows]
@@ -808,10 +875,13 @@
 
     @pl.when(here.xl == 0)
     def _():
-        unfold(z_send[...])
+        unfold(own_grad)
 
     @pl.when(here.xl == 1)
     def _():
+        z_send[...] = jnp.concatenate(
+            [own_grad[:, : middle // 2], own_grad[:, middle // 2 :]], axis=0
+        ).astype(BF16)
         for d in range(1, nz):
             remote(
                 z_send, z_recv.at[here.z], tail_sem.at[6], tail_sem.at[7], here.at_z(d)
@@ -819,10 +889,11 @@
         ref = z_recv.at[pl.ds(0, nz - 1)]
         gathered = remote(ref, ref, tail_sem.at[6], tail_sem.at[7], here.sibling())
         gathered.wait_recv()
-        clips = z_send[...]
-        for d in range(1, nz):
-            clips = clips + z_recv[here.up_z(d)]
-        unfold(clips / nz)
+        others = z_recv[here.up_z(1)].astype(F32)
+        for d in range(2, nz):
+            others = others + z_recv[here.up_z(d)].astype(F32)
+        few = 2 * own_rows
+        unfold((own_grad + jnp.concatenate([others[:few], others[few:]], axis=1)) / nz)
         gathered.wait_send()
 
     cross.wait_send()
@@ -840,6 +911,11 @@
     for three in rings:
         for ring in three:
             ring.finish()
+
+
+def hand_over(guided_in, grad_in, guided_ref, grad_ref):
+    guided_ref[...] = guided_in[...]
+    grad_ref[...] = grad_in[...]
 
 
 def on_device(
@@ -877,19 +953,25 @@
     dma = pltpu.SemaphoreType.DMA
     vmem = pl.BlockSpec(memory_space=pltpu.VMEM)
     smem = pl.BlockSpec(memory_space=pltpu.SMEM)
-    vectors = jnp.stack(
-        [cross_gain, cross_bias, q_gain, k_gain, jnp.pad(head_bias, (0, width - patch))]
-        + [jnp.zeros_like(k_gain)] * 3
-    )
     guided, grad = pl.pallas_call(
         kernel,
         out_shape=(
             jax.ShapeDtypeStruct((patch, count), F32),
             jax.ShapeDtypeStruct((own_rows, width), F32),
         ),
-        in_specs=[smem, smem] + [vmem] * 11,
+        in_specs=[smem, smem]
+        + [pl.BlockSpec(memory_space=pl.ANY)] * 4
+        + [vmem] * 4
+        + [pl.BlockSpec(memory_space=pl.ANY)] * 5
+        + [vmem]
+        + [pl.BlockSpec(memory_space=pl.ANY)],
         out_specs=(vmem, vmem),
         scratch_shapes=[
+            pltpu.VMEM((count, width), BF16),
+            pltpu.VMEM((text_rows, width), BF16),
+            pltpu.VMEM(head_mod.shape, F32),
+            pltpu.VMEM((patch, width), BF16),
+            pltpu.VMEM((patch, count), BF16),
             pltpu.VMEM((2, ny, 2, 2, rows, width), BF16),
             pltpu.VMEM((2, 2, 2, 2, rows, width), BF16),
             pltpu.VMEM((ny, 2, 2, 2 * rows, text_rows), BF16),
@@ -918,12 +1000,13 @@
             pltpu.VMEM((2, 2, eighth, wide), F32),
             pltpu.VMEM((2, eighth, wide), F32),
             pltpu.VMEM((eighth, width), F32),
+            pltpu.VMEM((1, width), F32),
             pltpu.VMEM((pairs, 2 * own_rows, middle), F32),
             pltpu.VMEM((pairs, 2 * own_rows, middle), F32),
             pltpu.VMEM((pairs, 2 * own_rows, middle + LANES), F32),
             pltpu.VMEM((pairs, 2 * own_rows, middle + LANES), F32),
-            pltpu.VMEM((2 * own_rows, middle), F32),
-            pltpu.VMEM((nz, 2 * own_rows, middle), F32),
+            pltpu.VMEM((4 * own_rows, middle // 2), BF16),
+            pltpu.VMEM((nz, 4 * own_rows, middle // 2), BF16),
             dma((4 * ny,)),
             dma((3,)),
             dma((2, 4 * ny)),
@@ -939,6 +1022,7 @@
             dma((ny,)),
             dma((pairs,)),
             dma((8,)),
+            dma((14,)),
         ],
         compiler_params=pltpu.CompilerParams(
             collective_id=0, has_side_effects=True, vmem_limit_bytes=60 * 1024 * 1024
@@ -953,14 +1037,27 @@
         prompt[0],
         null_embed,
         head_mod,
-        vectors,
+        cross_gain,
+        cross_bias,
+        q_gain,
+        k_gain,
         w_query.T,
         w_key.T,
         w_value.T,
         w_out.T,
         w_head.T,
+        head_bias,
         target[0].T,
     )
+    guided, grad = pl.pallas_call(
+        hand_over,
+        out_shape=(
+            jax.ShapeDtypeStruct((patch, count), F32),
+            jax.ShapeDtypeStruct((own_rows, width), F32),
+        ),
+        in_specs=[vmem, vmem],
+        out_specs=(vmem, vmem),
+    )(guided, grad)
     return (guided.T[None], grad.reshape(1, 1, own_rows, width))
 
 

time: 121 us -> 108 us (0.89)
  local copies, waits for them, and re-layouts: 7.06 us -> 0 us
  Pallas kernels: 112 us -> 106 us
    pallas_call x1, Pallas kernels: 112 us -> 105 us  [on_device(): pl.pallas_call(kernel, out_shape=(jax.ShapeDtypeStruct((patch, count), F3...]
    another operation x8 -> x0, local copies, waits for them, and re-layouts: 3.51 us -> none  [on_device(): jnp.stack([cross_gain, cross_bias, q_gain, k_gain, jnp.pad(head_bias, (0,...]
    unnamed x2 -> x0, local copies, waits for them, and re-layouts: 2.89 us -> none
    pallas_call x0 -> x1, Pallas kernels: none -> 1.55 us  [on_device(): pl.pallas_call(hand_over, out_shape=(jax.ShapeDtypeStruct((patch, count),...]
where the time goes in v3:
time: 108 us
  Pallas kernels  106 us (98%)
  between operations  1.94 us (2%)
    pallas_call x1, Pallas kernels, on_device(): pl.pallas_call(kernel, out_shape=(jax.ShapeDtypeStruct((patch, count), F3...  105 us

profile of v3, /device:TPU:6, one launch (start us, length us, event | category | flops | bytes accessed | tf_op | source)
XLA Modules:
  0.0 108.2 jit_solution(731439868708595268)
XLA Ops:
  1.9 104.7 %shard_map.176 = (f32[64,384]{1,0:T(8,128)}, f32[4,1536]{1,0:T(4,128)}) custom-call(s32[1]{0:T(128)S(6)} %copy.19.length_ref, s32[1]{0:T(128)S(6)} %copy.20.step_ref, bf16[384,1536]{1,0:T(8,128)(2,1)} %bitcast.14, bf16[128,1536]{1,0:T(8,128)(2,1)} %bitcast.15, bf16[128,1536]{1,0:T(8,128)(2,1)} %null_in.1, f32[50,2,1536]{2,1,0:T(2,128)} %head_mod_in.1, ...), custom_call_target="tpu_custom_call" | custom-call | flops 7247757312 | bytes 4718592 | tf_op jit(solution)/shard_map/pallas_call | solution.py:956
  106.7 1.5 %shard_map.177 = (f32[64,384]{1,0:T(8,128)}, f32[4,1536]{1,0:T(4,128)}) custom-call(f32[64,384]{1,0:T(8,128)} %get-tuple-element.6.guided_in, f32[4,1536]{1,0:T(4,128)} %get-tuple-element.7.grad_in), custom_call_target="tpu_custom_call" | custom-call | tf_op jit(solution)/shard_map/pallas_call | solution.py:1052

commit v4 on v3

--- a/solution.py
+++ b/solution.py
@@ -260,14 +260,17 @@
     def start(self):
         here = self.here
         self.copy(self.parity, here.xh, here.c, 2, here.other_columns()).start()
-        self.copy(self.parity, here.xh, here.c, 0, self.other_y).start()
         self.copy(self.parity, here.xh, here.c, 1, here.sibling()).start()
 
     def over_x(self):
         here = self.here
         self.copy(self.parity, 1 - here.xh, here.c, 2, here.other_columns()).wait_recv()
-        self.copy(self.parity, 1 - here.xh, here.c, 0, self.other_y).start()
         self.copy(self.parity, 1 - here.xh, here.c, 1, here.sibling()).start()
+
+    def begin_y(self):
+        here = self.here
+        for xh in (here.xh, 1 - here.xh):
+            self.copy(self.parity, xh, here.c, 0, self.other_y).start()
 
     def over_y(self):
         here = self.here
@@ -293,6 +296,10 @@
 
 def down(values):
     return jnp.sum(values, axis=0, keepdims=True)
+
+
+def gather_down(values):
+    return jnp.sum(values.reshape(values.shape[0] // 8, 8, values.shape[1]), axis=0)
 
 
 def dot(left, right):
@@ -365,8 +372,6 @@
     d_sibling,
     y_send,
     y_recv,
-    x_send,
-    x_recv,
     product,
     lane_gain,
     unit_send,
@@ -414,6 +419,7 @@
 
     partners = [here.sibling(), here.other_columns(), here.other_tokens(), here.other_branch()]
     partners += [here.at_y(d) for d in range(1, ny)] + [here.at_z(d) for d in range(1, nz)]
+    partners += [here.device(y=here.up_y(d), xh=1 - here.xh) for d in range(1, ny)]
     barrier = pltpu.get_barrier_semaphore()
     for device in partners:
         pl.semaphore_signal(barrier, inc=1, device_id=device, device_id_type=MESH)
@@ -543,10 +549,11 @@
         for t in range(token_blocks):
             lanes = slice(t * LANES, (t + 1) * LANES)
             tokens[at, lanes] = latents[lanes, at].T
-        return total + down(tokens[at, :].astype(F32))
-
-    zero_row = jnp.zeros((1, token_count), F32)
-    mean = lax.fori_loop(0, blocks, turn, zero_row) / width
+        return total + gather_down(tokens[at, :].astype(F32))
+
+    zero_row = jnp.zeros((8, token_count), F32)
+    unroll = 4 if blocks % 4 == 0 else 1
+    mean = down(lax.fori_loop(0, blocks, turn, zero_row, unroll=unroll)) / width
 
     small_round(QUERY, 1)
     text_ring.over_x()
@@ -555,9 +562,10 @@
 
     def spread(block, total):
         centred = tokens[rows_of(block, LANES), :].astype(F32) - mean
-        return total + down(centred * centred)
-
-    inverse = lax.rsqrt(lax.fori_loop(0, blocks, spread, zero_row) / width + NORM_EPS)
+        return total + gather_down(centred * centred)
+
+    variance = down(lax.fori_loop(0, blocks, spread, zero_row, unroll=unroll)) / width
+    inverse = lax.rsqrt(variance + NORM_EPS)
 
     def normalise(block, carry):
         at = rows_of(block, LANES)
@@ -570,9 +578,10 @@
     if pairs > 1:
         small_round(QUERY, 2)
     text_ring.round(1)
-    lax.fori_loop(0, blocks, normalise, 0)
+    lax.fori_loop(0, blocks, normalise, 0, unroll=unroll)
 
     y_out.start()
+    key_value.start()
     for k in range(3, pairs + 1):
         small_round(QUERY, k)
         small_round(OUT, k - 2)
@@ -601,6 +610,7 @@
     else:
         y_out.round(1)
     go_four(QUERY, 2)
+    key_value.over_x()
     for y in range(ny):
         text_ring.from_sibling(y)
 
@@ -614,19 +624,20 @@
         key_normed[h] = (one * key_inverse * columns[lanes, 3:4]).T.astype(BF16)
         value_rows[h] = values[lanes].T.astype(BF16)
 
+    go_four(OUT, 1)
     all_here(QUERY)
 
-    def project(y, total):
-        raw = dot(weights[QUERY, y].reshape(band, width), cross_in[...])
-        query_raw[rows_of(y, band), :] = raw
-        return total + down(raw * raw)
-
-    square = lax.fori_loop(0, ny // 2, project, zero_row)
-    go_four(OUT, 1)
+    def project(i, total):
+        raw = dot(weights[QUERY, pl.ds(i * 2, 2)].reshape(2 * band, width), cross_in[...])
+        query_raw[rows_of(i, 2 * band), :] = raw
+        return total + gather_down(raw * raw)
+
+    square = lax.fori_loop(0, pairs // 2, project, zero_row)
     if pairs > 2:
         y_out.round(3)
-    square = lax.fori_loop(ny // 2, ny, project, square)
-    query_inverse = lax.rsqrt(square / width + NORM_EPS)
+    key_value.begin_y()
+    square = lax.fori_loop(pairs // 2, pairs, project, square)
+    query_inverse = lax.rsqrt(down(square) / width + NORM_EPS)
 
     length = here.xl * text_rows + (1 - here.xl) * length_ref[0]
     visible = text_row(lax.broadcasted_iota(jnp.int32, (text_rows, token_count), 0)) < length
@@ -652,40 +663,85 @@
     lax.fori_loop(heads // 4, heads // 2, attend, 0, unroll=True)
     if pairs > 3:
         y_out.round(4)
-    key_value.start()
     lax.fori_loop(heads // 2, heads, attend, 0, unroll=True)
     all_here(OUT)
 
-    def project_out(y, total):
-        at = rows_of(y, band)
-        rows_after = dot(weights[OUT, y].reshape(band, width), attended[...]) + tokens[at, :].astype(F32)
-        after[at, :] = rows_after
-        return total + down(rows_after)
-
-    head_mean = lax.fori_loop(0, ny, project_out, zero_row) / width
-
-    def head_spread(block, total):
-        centred = after[rows_of(block, LANES), :] - head_mean
-        return total + down(centred * centred)
-
-    head_inverse = lax.rsqrt(lax.fori_loop(0, blocks, head_spread, zero_row) / width + NORM_EPS)
-
-    def modulate(block, carry):
-        at = rows_of(block, LANES)
-        unit = (after[at, :] - head_mean) * head_inverse
-        head_in[at, :] = (unit * columns[at, 4:5] + columns[at, 5:6]).astype(BF16)
-        return carry
-
-    lax.fori_loop(0, blocks, modulate, 0)
-    noise[here.xl] = dot(w_head[...], head_in[...]) + columns[:patch, 6:7]
-
-    def swap(branch):
-        ref = noise.at[branch]
-        return remote(ref, ref, swap_sem.at[0], swap_sem.at[1], here.other_branch())
-
-    swap(here.xl).start()
-    key_value.over_x()
-
+    cutting = (token_blocks + 1) // 2 * LANES
+    parts = [slice(0, cutting)] + ([slice(cutting, token_count)] if cutting < token_count else [])
+
+    def swap(number, branch):
+        ref = noise.at[branch, :, parts[number]]
+        return remote(
+            ref, ref, swap_sem.at[0, number], swap_sem.at[1, number], here.other_branch()
+        )
+
+    def head_forward(number):
+        lanes = parts[number]
+        start = jnp.zeros((8, lanes.stop - lanes.start), F32)
+
+        def project_out(i, total):
+            at = rows_of(i, 2 * band)
+            matrix = weights[OUT, pl.ds(i * 2, 2)].reshape(2 * band, width)
+            rows_after = dot(matrix, attended[:, lanes]) + tokens[at, lanes].astype(F32)
+            after[at, lanes] = rows_after
+            return total + gather_down(rows_after)
+
+        head_mean = down(lax.fori_loop(0, pairs, project_out, start)) / width
+
+        def head_spread(block, total):
+            centred = after[rows_of(block, LANES), lanes] - head_mean
+            return total + gather_down(centred * centred)
+
+        variance = down(lax.fori_loop(0, blocks, head_spread, start, unroll=unroll)) / width
+        head_inverse = lax.rsqrt(variance + NORM_EPS)
+
+        def modulate(block, carry):
+            at = rows_of(block, LANES)
+            unit = (after[at, lanes] - head_mean) * head_inverse
+            head_in[at, lanes] = (unit * columns[at, 4:5] + columns[at, 5:6]).astype(BF16)
+            return carry
+
+        lax.fori_loop(0, blocks, modulate, 0, unroll=unroll)
+        noise[here.xl, :, lanes] = dot(w_head[...], head_in[:, lanes]) + columns[:patch, 6:7]
+        swap(number, here.xl).start()
+        return head_mean, head_inverse
+
+    factor = GUIDE_SCALE - (2.0 * GUIDE_SCALE - 1.0) * here.xl.astype(F32)
+
+    def head_backward(number, head_mean, head_inverse):
+        lanes = parts[number]
+        start = jnp.zeros((8, lanes.stop - lanes.start), F32)
+        swap(number, 1 - here.xl).wait_recv()
+        cond, null = noise[0, :, lanes], noise[1, :, lanes]
+        guided = null + GUIDE_SCALE * (cond - null)
+        guided_ref[:, lanes] = guided
+        d_noise = (factor * (guided - target[:, lanes].astype(F32))).astype(BF16)
+
+        def head_back(block, sums):
+            at = rows_of(block, LANES)
+            unit = (after[at, lanes] - head_mean) * head_inverse
+            part_unit = dot(w_head_rows[at, :], d_noise) * columns[at, 4:5]
+            d_unit[at, lanes] = part_unit
+            return (sums[0] + gather_down(part_unit), sums[1] + gather_down(part_unit * unit))
+
+        first_sum, second_sum = lax.fori_loop(
+            0, blocks, head_back, (start, start), unroll=unroll
+        )
+        first_mean, second_mean = down(first_sum) / width, down(second_sum) / width
+
+        def norm_back(block, carry):
+            at = rows_of(block, LANES)
+            unit = (after[at, lanes] - head_mean) * head_inverse
+            grads = (head_inverse * (d_unit[at, lanes] - first_mean - unit * second_mean)).astype(
+                BF16
+            )
+            for t in range(lanes.start, lanes.stop, LANES):
+                d_after[t : t + LANES, at] = grads[:, t - lanes.start : t - lanes.start + LANES].T
+            return carry
+
+        lax.fori_loop(0, blocks, norm_back, 0, unroll=unroll)
+
+    stats = [head_forward(number) for number in range(len(parts))]
     def fold(values):
         return jnp.concatenate([values[:, :middle], values[:, middle:]], axis=0)
 
@@ -735,33 +791,8 @@
             total = total + recv[lax.rem(pair + d, pairs)]
         return total
 
-    swap(1 - here.xl).wait_recv()
-    swap(here.xl).wait_send()
-    guided = noise[1] + GUIDE_SCALE * (noise[0] - noise[1])
-    guided_ref[...] = guided
-    factor = GUIDE_SCALE - (2.0 * GUIDE_SCALE - 1.0) * here.xl.astype(F32)
-    d_noise = (factor * (guided - target[...].astype(F32))).astype(BF16)
-
-    def head_back(block, sums):
-        at = rows_of(block, LANES)
-        unit = (after[at, :] - head_mean) * head_inverse
-        part_unit = dot(w_head_rows[at, :], d_noise) * columns[at, 4:5]
-        d_unit[at, :] = part_unit
-        return (sums[0] + down(part_unit), sums[1] + down(part_unit * unit))
-
-    first_sum, second_sum = lax.fori_loop(0, blocks, head_back, (zero_row, zero_row))
-    first_mean, second_mean = first_sum / width, second_sum / width
-
-    def norm_back(block, carry):
-        at = rows_of(block, LANES)
-        unit = (after[at, :] - head_mean) * head_inverse
-        grads = (head_inverse * (d_unit[at, :] - first_mean - unit * second_mean)).astype(BF16)
-        for t in range(token_blocks):
-            lanes = slice(t * LANES, (t + 1) * LANES)
-            d_after[lanes, at] = grads[:, lanes].T
-        return carry
-
-    lax.fori_loop(0, blocks, norm_back, 0)
+    for number, (head_mean, head_inverse) in enumerate(stats):
+        head_backward(number, head_mean, head_inverse)
 
     def out_back(block, carry):
         at = rows_of(block, 2 * LANES)
@@ -769,7 +800,7 @@
         d_attended[:, at] = dot(d_after[...], matrix).astype(BF16)
         return carry
 
-    lax.fori_loop(0, blocks // 2, out_back, 0)
+    lax.fori_loop(0, blocks // 2, out_back, 0, unroll=2)
     key_value.over_y()
 
     def attend_back(h, carry):
@@ -798,15 +829,15 @@
             here.sibling(),
         )
 
-    def to_row(i, odd):
+    def to_row(i, odd, xh):
         lanes = rows_of(group(i), wide)
-        span = pl.ds(pl.multiple_of(odd * quarter, quarter), quarter)
+        span = pl.ds(pl.multiple_of(odd * quarter + xh * eighth, eighth), eighth)
         return remote(
             y_send.at[:, span, lanes],
-            y_recv.at[here.y],
+            y_recv.at[here.y, here.xh],
             y_send_sem.at[i],
-            y_recv_sem.at[here.y],
-            here.device(y=group(i) * 2 + odd),
+            y_recv_sem.at[here.y * 2 + here.xh],
+            here.device(y=group(i) * 2 + odd, xh=xh),
         )
 
     def sum_cores(i):
@@ -816,9 +847,12 @@
         y_send[:, :, lanes] = both.astype(BF16)
         if i < pairs - 1:
             for odd in (0, 1):
-                to_row(i, jnp.int32(odd)).start()
+                for xh in (0, 1):
+                    to_row(i, jnp.int32(odd), jnp.int32(xh)).start()
         else:
-            to_row(i, 1 - parity).start()
+            to_row(i, 1 - parity, here.xh).start()
+            to_row(i, 1 - parity, 1 - here.xh).start()
+            to_row(i, parity, 1 - here.xh).start()
             d_sibling[:, :, lanes] = both
 
     for i in range(pairs):
@@ -835,26 +869,24 @@
             units = exchange(unit_send, unit_recv, 2)
     sum_cores(pairs - 1)
 
-    quarter_span = pl.ds(pl.multiple_of(parity * quarter, quarter), quarter)
-    summed = d_sibling[:, quarter_span, own_lanes]
-    for d in list(range(2, ny)) + [0]:
-        y = lax.rem(pair * 2 + d, ny) if d else here.y + 1 - 2 * parity
-        ref = y_recv.at[y]
-        remote(ref, ref, y_send_sem.at[0], y_recv_sem.at[y], here.sibling()).wait_recv()
-        summed = summed + y_recv[y].astype(F32)
-    x_send[0] = summed[:, :eighth]
-    x_send[1] = summed[:, eighth:]
-    cross = remote(
-        x_send.at[1 - here.xh], x_recv, tail_sem.at[0], tail_sem.at[1], here.other_tokens()
+    eighth_span = pl.ds(
+        pl.multiple_of(parity * quarter + here.xh * eighth, eighth), eighth
     )
-    cross.start()
+    own_sum = d_sibling[:, eighth_span, own_lanes]
+    near_y = here.y + 1 - 2 * parity
+    sources = [(lax.rem(pair * 2 + d, ny), xh) for d in range(2, ny) for xh in (0, 1)]
+    sources += [(here.y, 1 - here.xh), (near_y, here.xh), (near_y, 1 - here.xh)]
+    for y, xh in sources:
+        ref = y_recv.at[y, xh]
+        remote(
+            ref, ref, y_send_sem.at[0], y_recv_sem.at[y * 2 + xh], here.sibling()
+        ).wait_recv()
+        own_sum = own_sum + y_recv[y, xh].astype(F32)
     if pairs > 1:
         units.wait_recv()
     unit_total = collect(unit_send, unit_recv)
     lane_gain[...] = row(k_gain)
     own_gain = lane_gain[:, own_lanes]
-    cross.wait_recv()
-    own_sum = x_send[here.xh] + x_recv[...]
     gained = own_sum[0] * own_gain
     statistic = jnp.sum(gained * near_unit, axis=-1, keepdims=True) / width
     multiply(jnp.concatenate([near_inverse * gained, own_sum[1]], axis=1), True)
@@ -896,7 +928,8 @@
         unfold((own_grad + jnp.concatenate([others[:few], others[few:]], axis=1)) / nz)
         gathered.wait_send()
 
-    cross.wait_send()
+    for number in range(len(parts)):
+        swap(number, here.xl).wait_send()
     if pairs > 1:
         units.wait_send()
         grads.wait_send()
@@ -904,7 +937,7 @@
         to_sibling(i).wait_send()
         ref = y_send.at[:, :, rows_of(group(i), wide)]
         if i == pairs - 1:
-            ref = y_send.at[:, pl.ds(0, quarter), rows_of(group(i), wide)]
+            ref = y_send.at[:, pl.ds(0, 3 * eighth), rows_of(group(i), wide)]
         remote(ref, ref, y_send_sem.at[i], y_recv_sem.at[0], here.sibling()).wait_send()
     text_ring.finish()
     key_value.finish()
@@ -996,9 +1029,7 @@
             pltpu.VMEM((2, text_rows, width), F32),
             pltpu.VMEM((2, half, width), F32),
             pltpu.VMEM((2, half, width), BF16),
-            pltpu.VMEM((ny, 2, quarter, wide), BF16),
-            pltpu.VMEM((2, 2, eighth, wide), F32),
-            pltpu.VMEM((2, eighth, wide), F32),
+            pltpu.VMEM((ny, 2, 2, eighth, wide), BF16),
             pltpu.VMEM((eighth, width), F32),
             pltpu.VMEM((1, width), F32),
             pltpu.VMEM((pairs, 2 * own_rows, middle), F32),
@@ -1017,9 +1048,9 @@
             dma((2, 3)),
             dma((8,)),
             dma((3,)),
-            dma((2,)),
+            dma((2, 2)),
             dma((2, pairs)),
-            dma((ny,)),
+            dma((2 * ny,)),
             dma((pairs,)),
             dma((8,)),
             dma((14,)),

time: 108 us -> 104 us (0.963)
  Pallas kernels: 106 us -> 101 us
    pallas_call x1, Pallas kernels: 105 us -> 99.9 us  [on_device(): pl.pallas_call(kernel, out_shape=(jax.ShapeDtypeStruct((patch, count), F3...]
where the time goes in v4:
time: 104 us; the launch traced here: 103 us
  Pallas kernels  101 us (97%)
  between operations  1.94 us (2%)
    pallas_call x1, Pallas kernels, on_device(): pl.pallas_call(kernel, out_shape=(jax.ShapeDtypeStruct((patch, count), F3...  99.9 us

profile of v4, /device:TPU:6, one launch (start us, length us, event | category | flops | bytes accessed | tf_op | source)
XLA Modules:
  0.0 103.4 jit_solution(4334862630800243353)
XLA Ops:
  1.9 99.9 %shard_map.176 = (f32[64,384]{1,0:T(8,128)}, f32[4,1536]{1,0:T(4,128)}) custom-call(s32[1]{0:T(128)S(6)} %copy.19.length_ref, s32[1]{0:T(128)S(6)} %copy.20.step_ref, bf16[384,1536]{1,0:T(8,128)(2,1)} %bitcast.14, bf16[128,1536]{1,0:T(8,128)(2,1)} %bitcast.15, bf16[128,1536]{1,0:T(8,128)(2,1)} %null_in.1, f32[50,2,1536]{2,1,0:T(2,128)} %head_mod_in.1, ...), custom_call_target="tpu_custom_call" | custom-call | flops 7247757312 | bytes 4718592 | tf_op jit(solution)/shard_map/pallas_call | solution.py:989
  101.8 1.5 %shard_map.177 = (f32[64,384]{1,0:T(8,128)}, f32[4,1536]{1,0:T(4,128)}) custom-call(f32[64,384]{1,0:T(8,128)} %get-tuple-element.6.guided_in, f32[4,1536]{1,0:T(4,128)} %get-tuple-element.7.grad_in), custom_call_target="tpu_custom_call" | custom-call | tf_op jit(solution)/shard_map/pallas_call | solution.py:1083

commit v5 on v4

--- a/solution.py
+++ b/solution.py
@@ -413,7 +413,7 @@
     own_rows = share // 4
     half, quarter, eighth = text_rows // 2, text_rows // 4, text_rows // 8
     wide = width // pairs
-    middle = width // 2
+    middle = width // 4
     parity = lax.rem(here.y, 2)
     pair = lax.div(here.y, 2)
 
@@ -743,7 +743,9 @@
 
     stats = [head_forward(number) for number in range(len(parts))]
     def fold(values):
-        return jnp.concatenate([values[:, :middle], values[:, middle:]], axis=0)
+        return jnp.concatenate(
+            [values[:, q * middle : (q + 1) * middle] for q in range(4)], axis=0
+        )
 
     def split(values):
         high = values.astype(BF16)
@@ -770,7 +772,7 @@
             product[:, at] = result[:eighth] + result[eighth:]
             return carry
 
-        lax.fori_loop(0, blocks // 2, columns_of, 0)
+        lax.fori_loop(0, blocks // 2, columns_of, 0, unroll=2)
 
     def exchange(send, recv, lane):
         for d in range(1, pairs):
@@ -786,9 +788,9 @@
         return remote(ref, ref, tail_sem.at[lane], tail_sem.at[lane + 1], here.sibling())
 
     def collect(send, recv):
-        total = send[pair]
+        total = send[pair].astype(F32)
         for d in range(1, pairs):
-            total = total + recv[lax.rem(pair + d, pairs)]
+            total = total + recv[lax.rem(pair + d, pairs)].astype(F32)
         return total
 
     for number, (head_mean, head_inverse) in enumerate(stats):
@@ -892,18 +894,22 @@
     multiply(jnp.concatenate([near_inverse * gained, own_sum[1]], axis=1), True)
     for q in range(pairs):
         span = slice(q * own_rows, (q + 1) * own_rows)
-        grad_send[q, :, :middle] = fold(product[span, :])
+        grad_send[q, :, :middle] = fold(product[span, :]).astype(BF16)
         both = jnp.broadcast_to(statistic[span], (own_rows, LANES))
-        grad_send[q, :, middle:] = jnp.concatenate([both, both], axis=0)
+        rounded = both.astype(BF16).astype(F32)
+        low_half = lax.broadcasted_iota(jnp.int32, (own_rows, LANES), 1) < LANES // 2
+        both = jnp.where(low_half, rounded, both - rounded)
+        grad_send[q, :, middle:] = jnp.concatenate([both] * 4, axis=0).astype(BF16)
     grads = exchange(grad_send, grad_recv, 4)
     if pairs > 1:
         grads.wait_recv()
     total = collect(grad_send, grad_recv)
-    own_grad = total[:, :middle] - total[:, middle : middle + 1] * unit_total
+    both = total[:, middle : middle + 1] + total[:, middle + LANES // 2 : middle + LANES // 2 + 1]
+    own_grad = total[:, :middle] - both * unit_total
 
     def unfold(values):
-        grad_ref[:, :middle] = values[:own_rows]
-        grad_ref[:, middle:] = values[own_rows:]
+        for q in range(4):
+            grad_ref[:, q * middle : (q + 1) * middle] = values[q * own_rows : (q + 1) * own_rows]
 
     @pl.when(here.xl == 0)
     def _():
@@ -911,9 +917,7 @@
 
     @pl.when(here.xl == 1)
     def _():
-        z_send[...] = jnp.concatenate(
-            [own_grad[:, : middle // 2], own_grad[:, middle // 2 :]], axis=0
-        ).astype(BF16)
+        z_send[...] = own_grad.astype(BF16)
         for d in range(1, nz):
             remote(
                 z_send, z_recv.at[here.z], tail_sem.at[6], tail_sem.at[7], here.at_z(d)
@@ -924,8 +928,7 @@
         others = z_recv[here.up_z(1)].astype(F32)
         for d in range(2, nz):
             others = others + z_recv[here.up_z(d)].astype(F32)
-        few = 2 * own_rows
-        unfold((own_grad + jnp.concatenate([others[:few], others[few:]], axis=1)) / nz)
+        unfold((own_grad + others) / nz)
         gathered.wait_send()
 
     for number in range(len(parts)):
@@ -946,9 +949,15 @@
             ring.finish()
 
 
-def hand_over(guided_in, grad_in, guided_ref, grad_ref):
-    guided_ref[...] = guided_in[...]
-    grad_ref[...] = grad_in[...]
+def hand_over(guided_in, grad_in, guided_ref, grad_ref, sem):
+    copies = [
+        pltpu.make_async_copy(guided_in, guided_ref, sem.at[0]),
+        pltpu.make_async_copy(grad_in, grad_ref, sem.at[1]),
+    ]
+    for copy in copies:
+        copy.start()
+    for copy in copies:
+        copy.wait()
 
 
 def on_device(
@@ -980,7 +989,7 @@
     heads = width // LANES
     pairs = ny // 2
     wide = width // pairs
-    middle = width // 2
+    middle = width // 4
     half, quarter, eighth = text_rows // 2, text_rows // 4, text_rows // 8
     own_rows = text_rows // ny // 4
     dma = pltpu.SemaphoreType.DMA
@@ -1032,12 +1041,12 @@
             pltpu.VMEM((ny, 2, 2, eighth, wide), BF16),
             pltpu.VMEM((eighth, width), F32),
             pltpu.VMEM((1, width), F32),
-            pltpu.VMEM((pairs, 2 * own_rows, middle), F32),
-            pltpu.VMEM((pairs, 2 * own_rows, middle), F32),
-            pltpu.VMEM((pairs, 2 * own_rows, middle + LANES), F32),
-            pltpu.VMEM((pairs, 2 * own_rows, middle + LANES), F32),
-            pltpu.VMEM((4 * own_rows, middle // 2), BF16),
-            pltpu.VMEM((nz, 4 * own_rows, middle // 2), BF16),
+            pltpu.VMEM((pairs, 4 * own_rows, middle), F32),
+            pltpu.VMEM((pairs, 4 * own_rows, middle), F32),
+            pltpu.VMEM((pairs, 4 * own_rows, middle + LANES), BF16),
+            pltpu.VMEM((pairs, 4 * own_rows, middle + LANES), BF16),
+            pltpu.VMEM((4 * own_rows, middle), BF16),
+            pltpu.VMEM((nz, 4 * own_rows, middle), BF16),
             dma((4 * ny,)),
             dma((3,)),
             dma((2, 4 * ny)),
@@ -1086,8 +1095,9 @@
             jax.ShapeDtypeStruct((patch, count), F32),
             jax.ShapeDtypeStruct((own_rows, width), F32),
         ),
-        in_specs=[vmem, vmem],
-        out_specs=(vmem, vmem),
+        in_specs=[pl.BlockSpec(memory_space=pl.ANY)] * 2,
+        out_specs=(pl.BlockSpec(memory_space=pl.ANY),) * 2,
+        scratch_shapes=[dma((2,))],
     )(guided, grad)
     return (guided.T[None], grad.reshape(1, 1, own_rows, width))
 

time: 104 us -> 105 us (level)
  Pallas kernels: 101 us -> 103 us
    pallas_call x1, Pallas kernels: 1.55 us -> 4.84 us  [on_device(): pl.pallas_call(hand_over, out_shape=(jax.ShapeDtypeStruct((patch, count),...]
    pallas_call x1, Pallas kernels: 99.9 us -> 98.2 us  [on_device(): pl.pallas_call(kernel, out_shape=(jax.ShapeDtypeStruct((patch, count), F3...]
where the time goes in v5:
time: 105 us
  Pallas kernels  103 us (98%)
  between operations  1.94 us (2%)
    pallas_call x1, Pallas kernels, on_device(): pl.pallas_call(kernel, out_shape=(jax.ShapeDtypeStruct((patch, count), F3...  98.2 us
    pallas_call x1, Pallas kernels, on_device(): pl.pallas_call(hand_over, out_shape=(jax.ShapeDtypeStruct((patch, count),...  4.84 us

profile of v5, /device:TPU:6, one launch (start us, length us, event | category | flops | bytes accessed | tf_op | source)
XLA Modules:
  0.0 105.0 jit_solution(16063396007461224639)
XLA Ops:
  1.9 98.2 %shard_map.176 = (f32[64,384]{1,0:T(8,128)}, f32[4,1536]{1,0:T(4,128)}) custom-call(s32[1]{0:T(128)S(6)} %copy.19.length_ref, s32[1]{0:T(128)S(6)} %copy.20.step_ref, bf16[384,1536]{1,0:T(8,128)(2,1)} %bitcast.14, bf16[128,1536]{1,0:T(8,128)(2,1)} %bitcast.15, bf16[128,1536]{1,0:T(8,128)(2,1)} %null_in.1, f32[50,2,1536]{2,1,0:T(2,128)} %head_mod_in.1, ...), custom_call_target="tpu_custom_call" | custom-call | flops 7247757312 | bytes 4718592 | tf_op jit(solution)/shard_map/pallas_call | solution.py:998
  100.2 4.8 %shard_map.177 = (f32[64,384]{1,0:T(8,128)}, f32[4,1536]{1,0:T(4,128)}) custom-call(f32[64,384]{1,0:T(8,128)} %get-tuple-element.6.guided_in, f32[4,1536]{1,0:T(4,128)} %get-tuple-element.7.grad_in), custom_call_target="tpu_custom_call" | custom-call | tf_op jit(solution)/shard_map/pallas_call | solution.py:1092

commit v6 on v5

--- a/solution.py
+++ b/solution.py
@@ -949,15 +949,9 @@
             ring.finish()
 
 
-def hand_over(guided_in, grad_in, guided_ref, grad_ref, sem):
-    copies = [
-        pltpu.make_async_copy(guided_in, guided_ref, sem.at[0]),
-        pltpu.make_async_copy(grad_in, grad_ref, sem.at[1]),
-    ]
-    for copy in copies:
-        copy.start()
-    for copy in copies:
-        copy.wait()
+def hand_over(guided_in, grad_in, guided_ref, grad_ref):
+    guided_ref[...] = guided_in[...]
+    grad_ref[...] = grad_in[...]
 
 
 def on_device(
@@ -1095,9 +1089,8 @@
             jax.ShapeDtypeStruct((patch, count), F32),
             jax.ShapeDtypeStruct((own_rows, width), F32),
         ),
-        in_specs=[pl.BlockSpec(memory_space=pl.ANY)] * 2,
-        out_specs=(pl.BlockSpec(memory_space=pl.ANY),) * 2,
-        scratch_shapes=[dma((2,))],
+        in_specs=[vmem, vmem],
+        out_specs=(vmem, vmem),
     )(guided, grad)
     return (guided.T[None], grad.reshape(1, 1, own_rows, width))
 

time: 105 us -> 102 us (0.971)
  Pallas kernels: 103 us -> 99.8 us
    pallas_call x1, Pallas kernels: 4.84 us -> 1.55 us  [on_device(): pl.pallas_call(hand_over, out_shape=(jax.ShapeDtypeStruct((patch, count),...]
where the time goes in v6:
time: 102 us
  Pallas kernels  99.8 us (98%)
  between operations  1.94 us (2%)
    pallas_call x1, Pallas kernels, on_device(): pl.pallas_call(kernel, out_shape=(jax.ShapeDtypeStruct((patch, count), F3...  98.2 us

profile of v6, /device:TPU:6, one launch (start us, length us, event | category | flops | bytes accessed | tf_op | source)
XLA Modules:
  0.0 101.7 jit_solution(8530910672336283353)
XLA Ops:
  1.9 98.2 %shard_map.176 = (f32[64,384]{1,0:T(8,128)}, f32[4,1536]{1,0:T(4,128)}) custom-call(s32[1]{0:T(128)S(6)} %copy.19.length_ref, s32[1]{0:T(128)S(6)} %copy.20.step_ref, bf16[384,1536]{1,0:T(8,128)(2,1)} %bitcast.14, bf16[128,1536]{1,0:T(8,128)(2,1)} %bitcast.15, bf16[128,1536]{1,0:T(8,128)(2,1)} %null_in.1, f32[50,2,1536]{2,1,0:T(2,128)} %head_mod_in.1, ...), custom_call_target="tpu_custom_call" | custom-call | flops 7247757312 | bytes 4718592 | tf_op jit(solution)/shard_map/pallas_call | solution.py:992
  100.2 1.5 %shard_map.177 = (f32[64,384]{1,0:T(8,128)}, f32[4,1536]{1,0:T(4,128)}) custom-call(f32[64,384]{1,0:T(8,128)} %get-tuple-element.6.guided_in, f32[4,1536]{1,0:T(4,128)} %get-tuple-element.7.grad_in), custom_call_target="tpu_custom_call" | custom-call | tf_op jit(solution)/shard_map/pallas_call | solution.py:1086
